TPU v7x, 32 devices: a whole 2x2x4 slice. The times are simulated.
32 devices in a mesh: ctx: 8 (over y, x, core), req: 4 (over z).
Axes of the slice: x: 2, y: 2, z: 4, core: 2. Of those that a mesh axis runs over, the one named last changes fastest.
Arguments:
- queries: bfloat16 [2048, 2048], P(('ctx', 'req')), may hold values from -20 to 20
- q_pos: int32 [2048], P(('ctx', 'req')), may hold values from 1 to 18431
- req_of: int32 [2048, 1], P(('ctx', 'req')), may hold values from 0 to 3; in each aligned block of 64 rows (0 to 63, 64 to 127, ...) at most 20 rows name the same one
- cache: bfloat16 [4, 18432, 256], P('req', 'ctx'), may hold values from -6 to 6
- cache_len: int32 [4], replicated, may hold values from 2 to 18432
Outputs:
- attended: bfloat16 [2048, 2048], P(('ctx', 'req'))
Inputs may be any that keep to these rules, and one draw needn't show every extreme that they name: `req_of`: no more than 20 of one device's 64 tokens name the same request, and some device's tokens reach 20 for some request.
All inputs are finite; a program needn't handle non-finite values.
Results may differ from a plain program's by a relative error of at most 0.006.
Values may be sent and summed in bfloat16 or wider, within the bound.
No kernel may reach another device: no remote copies, remote signals or barrier semaphores. Data moves between devices by JAX's collectives and lax.ppermute only.
A program may use at most 128 MiB of HBM per device.

v0:
```python
import functools
import math

import jax
import jax.numpy as jnp
from jax import lax
from jax.experimental import pallas as pl
from jax.experimental.pallas import tpu as pltpu
from jax.sharding import PartitionSpec as P

H = 16
HD = 128
WIDE = H * HD
META = 128
LOW = -1e30
TILE = 16
SUB = 256
OUT_ROWS = HD + 8
EXP_SCALE = HD**-0.5 * math.log2(math.e)
NT = (((1,), (1,)), ((), ()))
NN = (((1,), (0,)), ((), ()))
VMEM = pl.BlockSpec(memory_space=pltpu.VMEM)
SMEM = pl.BlockSpec(memory_space=pltpu.SMEM)


def dot(a, b, dims=NN):
    return lax.dot_general(a, b, dims, preferred_element_type=jnp.float32)


def iota(shape, dim):
    return lax.broadcasted_iota(jnp.int32, shape, dim)


def row_of(column):
    return jnp.transpose(jnp.broadcast_to(column, (column.shape[0], 128)), (1, 0))[:1, :]


def call(body, out_shape, in_specs, name, scratch=(), limit=48, aliases=None):
    many = isinstance(out_shape, list)
    return pl.pallas_call(
        body,
        out_shape=out_shape,
        in_specs=in_specs,
        out_specs=[VMEM] * len(out_shape) if many else VMEM,
        scratch_shapes=list(scratch),
        compiler_params=pltpu.CompilerParams(vmem_limit_bytes=limit << 20),
        cost_estimate=pl.CostEstimate(flops=1, bytes_accessed=1, transcendentals=0),
        input_output_aliases=aliases or {},
        name=name,
    )


def fold_of(capacity):
    fold = 1
    while capacity * fold % 8:
        fold *= 2
    return fold


def route_kernel(capacity, me_ref, req_ref, pos_ref, q_ref, *outs):
    sends, back_ref = outs[:-1], outs[-1]
    rows = q_ref.shape[0]
    fold = fold_of(capacity)
    block, width = capacity * fold, WIDE // fold
    target_c = req_ref[...]
    target_r = row_of(target_c.astype(jnp.float32)).astype(jnp.int32)
    same = target_c == target_r
    i0, i1 = iota((rows, rows), 0), iota((rows, rows), 1)
    rank_c = jnp.sum((same & (i1 < i0)).astype(jnp.int32), axis=1, keepdims=True)
    rank_r = jnp.sum((same & (i0 < i1)).astype(jnp.int32), axis=0, keepdims=True)
    slot_c = (target_c ^ me_ref[1]) * block + rank_c
    slot_r = (target_r ^ me_ref[1]) * block + rank_r
    total = len(sends) * block
    moved = jnp.zeros((total, width), jnp.float32)
    taken = jnp.zeros((total, rows), jnp.float32)
    for f in range(fold):
        back_ref[f] = (slot_c + f * capacity == iota((rows, total), 1)).astype(jnp.bfloat16)
        place = (slot_r + f * capacity == iota((total, rows), 0)).astype(jnp.float32)
        moved += dot(place.astype(jnp.bfloat16), q_ref[:, f * width : (f + 1) * width])
        taken += place
    plus = pos_ref[...] + 1
    high = jnp.sum(taken * (plus >> 8).astype(jnp.float32), axis=1, keepdims=True)
    low = jnp.sum(taken * (plus & 255).astype(jnp.float32), axis=1, keepdims=True)
    lane = iota((total, META), 1)
    meta = jnp.where(lane == 0, high, jnp.where(lane == 1, low, 0.0)).astype(jnp.bfloat16)
    moved = moved.astype(jnp.bfloat16)
    for d, out in enumerate(sends):
        out[:, :width] = moved[d * block : (d + 1) * block]
        out[:, width:] = meta[d * block : (d + 1) * block]


def row_parts(shape, dim, capacity):
    fold = fold_of(capacity)
    row = iota(shape, dim)
    token = jnp.zeros(shape, jnp.int32)
    part = jnp.zeros(shape, jnp.int32)
    for i in range(1, shape[dim] // capacity):
        passed = (row >= i * capacity).astype(jnp.int32)
        part += passed if i % fold else (1 - fold) * passed
    token = row - part * capacity
    for i in range(1, shape[dim] // (capacity * fold)):
        token -= (row >= i * capacity * fold).astype(jnp.int32) * (capacity * fold - capacity)
    return token, part


def sort_kernel(capacity, *refs):
    blocks, out, back_ref = refs[:-2], refs[-2], refs[-1]
    slots = out.shape[0]
    fold = fold_of(capacity)
    width = WIDE // fold
    joined = jnp.concatenate([b[...] for b in blocks], axis=0)
    total = joined.shape[0]
    meta = joined[:, width:].astype(jnp.float32)
    pos_c = meta[:, 0:1] * 256.0 + meta[:, 1:2]
    pos_r = row_of(pos_c)
    token_c, part_c = row_parts((total, 1), 0, capacity)
    token_r, part_r = row_parts((1, total), 1, capacity)
    ahead_r = ((pos_c > pos_r) | ((pos_c == pos_r) & (token_c < token_r))) & (part_c == 0)
    ahead_c = ((pos_r > pos_c) | ((pos_r == pos_c) & (token_r < token_c))) & (part_r == 0)
    rank_r = jnp.sum(ahead_r.astype(jnp.int32), axis=0, keepdims=True)
    rank_c = jnp.sum(ahead_c.astype(jnp.int32), axis=1, keepdims=True)
    place = rank_r == iota((slots, total), 0)
    for f in range(fold):
        mine = (place & (part_r == f)).astype(jnp.bfloat16)
        out[:, f * width : (f + 1) * width] = dot(mine, joined[:, :width]).astype(jnp.bfloat16)
        if f == 0:
            out[:, WIDE:] = dot(mine, joined[:, width:]).astype(jnp.bfloat16)
        back_ref[f] = ((rank_c == iota((total, slots), 1)) & (part_c == f)).astype(jnp.bfloat16)


def keys_kernel(first, count, *refs):
    pieces, k_ref, vt_ref = refs[:count], refs[-2], refs[-1]
    piece = pieces[0].shape[0]
    extra = vt_ref.shape[0] - HD
    ones = (iota((extra, piece), 0) == 0).astype(jnp.bfloat16)
    for i, ref in enumerate(pieces, first):
        at = slice(i * piece, (i + 1) * piece)
        k_ref[at, :HD] = ref[:, :HD]
        k_ref[at, HD:] = ref[:, :HD]
        vt_ref[:HD, at] = jnp.transpose(ref[:, HD:], (1, 0))
        vt_ref[HD:, at] = ones


def flash_kernel(
    first, chips, piece, me_ref, len_ref, pq_ref, k_ref, vt_ref, out_ref, q_ref, acc_ref, row_ref, s_ref, top_ref, job_ref, info_ref
):
    width = TILE * H
    all_width = out_ref.shape[1]
    tiles = all_width // width
    pieces, pairs = 4, 2
    length = len_ref[me_ref[1]]
    chip, core = me_ref[0] // 2, lax.rem(me_ref[0], 2)
    kept_at, away_at = chip * (4 * piece), (chips - 1 - chip) * (4 * piece) + piece
    rising = kept_at < away_at
    for pair, kept in enumerate((rising, jnp.logical_not(rising))):
        for k in range(2):
            info_ref[2 * pair + k] = jnp.where(kept, kept_at, away_at) + 2 * piece * k
            info_ref[pieces + 2 * pair + k] = jnp.where(kept, 0, 2) + jnp.where(core == k, 0, 1)
    meta = pq_ref[first * TILE : (first + tiles) * TILE, WIDE:].astype(jnp.float32)
    pos = meta[:, 0:1] * 256.0 + meta[:, 1:2] - 1.0
    last = jnp.minimum(pos, (length - 1).astype(jnp.float32))
    count = jnp.int32(0)
    for j in range(tiles):
        here = last[j * TILE : (j + 1) * TILE]
        top = jnp.max(here).astype(jnp.int32)
        for i in range(pairs):
            job_ref[count] = j * pairs + i
            count += (info_ref[2 * i] <= top).astype(jnp.int32)
        row_ref[0:1, j * width : (j + 1) * width] = jnp.concatenate([row_of(here)] * H, axis=1)
        rows = slice((first + j) * TILE, (first + j + 1) * TILE)
        for h in range(H):
            x = pq_ref[rows, h * HD : (h + 1) * HD].astype(jnp.float32) * EXP_SCALE
            high = x.astype(jnp.bfloat16)
            at = slice(j * width + h * TILE, j * width + (h + 1) * TILE)
            q_ref[at, :HD] = high
            q_ref[at, HD:] = (x - high.astype(jnp.float32)).astype(jnp.bfloat16)
    for k in range(3):
        job_ref[count + k] = tiles * pairs
    row_ref[0:1, all_width:] = jnp.full((1, width), -1.0, jnp.float32)
    q_ref[all_width:, :] = jnp.zeros((width, 2 * HD), jnp.bfloat16)
    acc_ref[...] = jnp.zeros_like(acc_ref)

    def place(job):
        tile = job // pairs
        return pl.ds(pl.multiple_of(tile * width, width), width), 2 * (job - tile * pairs)

    def keys(c, a, n):
        return pl.ds(pl.multiple_of(info_ref[pieces + c] * piece + a, 128), n)

    def scores(cols, c, a, n):
        return dot(k_ref[keys(c, a, n), :], q_ref[cols, :], NT)

    def masked(s, cols, c, a):
        limit = row_ref[0:1, cols].astype(jnp.int32) - (info_ref[c] + a)
        return jnp.where(iota(s.shape, 0) <= limit, s, LOW)

    subs = [(0, SUB), (SUB, piece - SUB)]

    @pl.when(count > 0)
    def _():
        for k in range(2):
            cols, c = place(job_ref[k])
            s_ref[k] = scores(cols, c, *subs[0])

    def turn(b, carry):
        now = [place(job_ref[2 * b + k]) for k in range(2)]
        later = [place(job_ref[2 * b + 2 + k]) for k in range(2)]
        steps = [(g, a, n) for g in range(2) for a, n in subs]
        s = [s_ref[k] for k in range(2)]
        totals = [None, None]
        for i, (g, a, n) in enumerate(steps):
            if i + 1 < len(steps):
                g2, a2, n2 = steps[i + 1]
                next_s = [scores(cols, c + g2, a2, n2) for cols, c in now]
            else:
                next_s = [scores(cols, c, *subs[0]) for cols, c in later]
            for k, (cols, c) in enumerate(now):
                weights = jnp.exp2(masked(s[k], cols, c + g, a)).astype(jnp.bfloat16)
                term = dot(vt_ref[:, keys(c + g, a, n)], weights)
                totals[k] = term if totals[k] is None else totals[k] + term
            s = next_s
        for k in range(2):
            s_ref[k] = s[k]
        for k, (cols, _) in enumerate(now):
            acc_ref[:, cols] += totals[k]
        return carry

    lax.fori_loop(0, (count + 1) // 2, turn, 0)
    top_ref[0:1, :] = jnp.zeros((1, all_width), jnp.float32)
    total = acc_ref[HD : HD + 1, :all_width]
    dead = row_ref[0:1, :all_width] < info_ref[0].astype(jnp.float32)
    fine = dead | ((total > 2.0**-60) & (total < 2.0**100))

    @pl.when(jnp.logical_not(jnp.min(fine.astype(jnp.float32)) > 0.5))
    def _():
        acc_ref[...] = jnp.zeros_like(acc_ref)
        top_ref[0:1, :] = jnp.full((1, all_width), 0.1 * LOW, jnp.float32)

        def careful(i, carry):
            chunks = piece // 128
            cols = pl.ds(pl.multiple_of(i // (pieces * chunks) * width, width), width)
            c, a = i % (pieces * chunks) // chunks, i % chunks * 128
            s = masked(scores(cols, c, a, 128), cols, c, a)
            before = top_ref[0:1, cols]
            after = jnp.maximum(before, jnp.max(s, axis=0, keepdims=True))
            weights = jnp.exp2(s - after).astype(jnp.bfloat16)
            acc_ref[:, cols] = acc_ref[:, cols] * jnp.exp2(before - after) + dot(vt_ref[:, keys(c, a, 128)], weights)
            top_ref[0:1, cols] = after
            return carry

        lax.fori_loop(0, tiles * pieces * (piece // 128), careful, 0)

    total = acc_ref[HD : HD + 1, :all_width]
    some = total > 0.0
    safe = jnp.where(some, total, 1.0)
    out_ref[:HD, :] = (acc_ref[:HD, :all_width] * (1.0 / safe)).astype(jnp.bfloat16)
    lse = jnp.where(some, top_ref[0:1, :] + jnp.log2(safe), LOW)
    a = lse.astype(jnp.bfloat16).astype(jnp.float32)
    b = (lse - a).astype(jnp.bfloat16).astype(jnp.float32)
    row = iota((OUT_ROWS - HD, all_width), 0)
    terms = jnp.where(row == 0, a, jnp.where(row == 1, b, jnp.where(row == 2, lse - a - b, 0.0)))
    out_ref[HD:, :] = terms.astype(jnp.bfloat16)


def merge_kernel(count, *refs):
    own, parts, back_ref, outs, slot_ref = refs[:2], refs[2 : count + 2], refs[count + 2], refs[count + 3 : -1], refs[-1]
    fold = back_ref.shape[0]
    width = TILE * H
    split = own[0].shape[1] // width
    for j in range(slot_ref.shape[0] // TILE):
        here = [(own[0], j) if j < split else (own[1], j - split)] + [(part, j) for part in parts]
        here = [(part, slice(i * width, (i + 1) * width)) for part, i in here]
        lses = [sum(part[HD + i : HD + i + 1, cols].astype(jnp.float32) for i in range(3)) for part, cols in here]
        high = functools.reduce(jnp.maximum, lses)
        shares = [jnp.exp2(lse - high) for lse in lses]
        scale = 1.0 / functools.reduce(jnp.add, shares)
        merged = sum((share * scale) * part[:HD, cols].astype(jnp.float32) for share, (part, cols) in zip(shares, here))
        merged = jnp.transpose(merged, (1, 0)).astype(jnp.bfloat16)
        for h in range(H):
            slot_ref[j * TILE : (j + 1) * TILE, h * HD : (h + 1) * HD] = merged[h * TILE : (h + 1) * TILE]
    block, cut = outs[0].shape
    placed = sum(dot(back_ref[f], slot_ref[:, f * cut : (f + 1) * cut]) for f in range(fold))
    placed = placed.astype(jnp.bfloat16)
    for d, out in enumerate(outs):
        out[...] = placed[d * block : (d + 1) * block]


def unroute_kernel(*refs):
    blocks, back_ref, out = refs[:-2], refs[-2], refs[-1]
    width = blocks[0].shape[1]
    joined = jnp.concatenate([b[...] for b in blocks], axis=0)
    for f in range(back_ref.shape[0]):
        out[:, f * width : (f + 1) * width] = dot(back_ref[f], joined).astype(jnp.bfloat16)


def swapped(block, axis, distance):
    devices = range(lax.axis_size(axis))
    return lax.ppermute(block, axis, [(i, i ^ distance) for i in devices])


def per_device(queries, q_pos, req_of, cache, cache_len):
    tok_rows = queries.shape[0]
    groups = lax.axis_size("req")
    cycle = lax.axis_size("ctx")
    chips = cycle // 2
    capacity = 5 * tok_rows // (4 * groups)
    slots = groups * capacity
    fold = fold_of(capacity)
    block, width = capacity * fold, WIDE // fold
    shard_len = cache.shape[1]
    half = shard_len // 2
    here = lax.axis_index("ctx")
    mine = lax.axis_index("req")
    me = jnp.stack([here, mine]).astype(jnp.int32)
    bf = lambda *shape: jax.ShapeDtypeStruct(shape, jnp.bfloat16)

    other = cycle - 2
    away = swapped(cache[0, half:], "ctx", other)

    *sends, back_tok = call(
        functools.partial(route_kernel, capacity),
        [bf(block, width + META)] * groups + [bf(fold, tok_rows, groups * block)],
        [SMEM] + [VMEM] * 3,
        "route",
    )(me, req_of, q_pos.reshape(1, tok_rows), queries)
    sends[0], kept = lax.optimization_barrier((sends[0], cache[0, :half]))
    blocks = [sends[0]] + [swapped(sends[d], "req", d) for d in range(1, groups)]
    kept_sib = swapped(kept, "ctx", 1)
    all_keys = [bf(4 * half, 2 * HD), bf(HD + 16, 4 * half)]
    kept_keys = call(functools.partial(keys_kernel, 0, 2), all_keys, [VMEM] * 2, "keys_kept")(kept, kept_sib)
    blocks[0], *kept_keys = lax.optimization_barrier((blocks[0], *kept_keys))

    sorted_q, back_slot = call(
        functools.partial(sort_kernel, capacity),
        [bf(slots, WIDE + META), bf(fold, groups * block, slots)],
        [VMEM] * groups,
        "sort",
    )(*blocks)
    visiting = {d: swapped(sorted_q, "ctx", 2 * d) for d in range(1, chips)}
    sorted_q, away = lax.optimization_barrier((sorted_q, away))
    away_sib = swapped(away, "ctx", 1)
    k_all, vt_all = call(
        functools.partial(keys_kernel, 2, 2), all_keys, [VMEM] * 4, "keys_away", aliases={2: 0, 3: 1}
    )(away, away_sib, *kept_keys)

    def flash(q, first=0, tiles=slots // TILE):
        extra = (tiles + 1) * TILE * H
        return call(
            functools.partial(flash_kernel, first, chips, half),
            bf(OUT_ROWS, tiles * TILE * H),
            [SMEM, SMEM] + [VMEM] * 3,
            "flash",
            scratch=[
                pltpu.VMEM((extra, 2 * HD), jnp.bfloat16),
                pltpu.VMEM((HD + 16, extra), jnp.float32),
                pltpu.VMEM((8, extra), jnp.float32),
                pltpu.VMEM((2, SUB, TILE * H), jnp.float32),
                pltpu.VMEM((8, tiles * TILE * H), jnp.float32),
                pltpu.SMEM((2 * tiles + 4,), jnp.int32),
                pltpu.SMEM((8,), jnp.int32),
            ],
        )(me, cache_len, q, k_all, vt_all)

    turn = flash(sorted_q, 0, 1)
    own = [turn]
    home = []
    for d in sorted(visiting, key=lambda d: (d & (d - 1) != 0, d)):
        turn, q = lax.optimization_barrier((turn, visiting[d]))
        turn = flash(q)
        if d == chips - 1:
            turn, *home = lax.optimization_barrier((turn, *home))
        home.append(swapped(turn, "ctx", 2 * d))
    turn, q = lax.optimization_barrier((turn, sorted_q))
    own.append(flash(q, 1, slots // TILE - 1))
    home = [*own, *home]
    outs = call(
        functools.partial(merge_kernel, len(home) - 2),
        [bf(block, width)] * groups,
        [VMEM] * (len(home) + 1),
        "merge",
        scratch=[pltpu.VMEM((slots, WIDE), jnp.bfloat16)],
    )(*home, back_slot)
    back = [outs[0]] + [swapped(outs[d], "req", d) for d in range(1, groups)]
    return call(unroute_kernel, bf(tok_rows, WIDE), [VMEM] * (groups + 1), "unroute")(*back, back_tok)


def solution(mesh):
    in_specs = (
        P(("ctx", "req"), None),
        P(("ctx", "req")),
        P(("ctx", "req"), None),
        P("req", "ctx", None),
        P(),
    )
    out_specs = P(("ctx", "req"), None)
    return jax.shard_map(
        per_device, mesh=mesh, in_specs=in_specs, out_specs=out_specs, check_vma=False
    )
```

profile of v0, /device:TPU:0, one launch (start us, length us, event | category | flops | bytes accessed | tf_op | source)
XLA Modules:
  0.0 362.0 jit_solution(13799610557758505476)
XLA Ops:
  0.0 0.8 copy.8.req_ref
  0.8 1.3 slice_bitcast_fusion
  2.1 0.1 pad_add_fusion.me_ref
  2.2 1.0 route.1
  3.2 0.5 collective-permute-start
  3.7 3.5 collective-permute-start.4
  7.2 1.6 collective-permute-start.1
  8.8 2.6 collective-permute-start.2
  11.4 0.2 collective-permute-start.3
  11.6 0.3 keys_kept.1
  12.0 7.1 %collective-permute-done.2.refs_2_ = bf16[40,1152]{1,0:T(8,128)(2,1)S(1)} collective-permute-done((bf16[40,1152]{1,0:T(8,128)(2,1)S(1)}, bf16[40,1152]{1,0:T(8,128)(2,1)S(1)}, u32[]{:S(2)}, u32[]{:S(2)}) %collective-permute-start.2) | collective-permute-done | bytes 92192 | tf_op jit(solution)/shard_map/ppermute | solution.py:298
  19.1 0.5 sort.1
  19.6 1.6 collective-permute-done.4.refs_0_
  21.2 1.7 collective-permute-start.6
  22.9 1.5 collective-permute-start.7
  24.4 0.3 collective-permute-start.8
  24.7 0.3 keys_away.1
  25.0 2.8 flash.5.refs_0_
  27.7 4.4 %collective-permute-done.6.pq_ref = bf16[80,2176]{1,0:T(8,128)(2,1)S(1)} collective-permute-done((bf16[80,2176]{1,0:T(8,128)(2,1)S(1)}, bf16[80,2176]{1,0:T(8,128)(2,1)S(1)}, u32[]{:S(2)}, u32[]{:S(2)}) %collective-permute-start.6) | collective-permute-done | bytes 348192 | tf_op jit(solution)/shard_map/ppermute | solution.py:298
  32.1 80.8 %flash.6 = bf16[136,1280]{1,0:T(8,128)(2,1)S(1)} custom-call(s32[2]{0:T(128)S(1)} %pad_add_fusion.me_ref, s32[4]{0:T(128)S(1)} %copy-done.1, bf16[80,2176]{1,0:T(8,128)(2,1)S(1)} %collective-permute-done.6.pq_ref, bf16[4608,256]{1,0:T(8,128)(2,1)S(1)} %get-tuple-element.48.k_ref, bf16[144,4608]{1,0:T(8,128)(2,1)S(1)} %get-tuple-element.49.vt_ref), custom_call_target="tpu_custom_call" | custom-call | flops 1 | bytes 1 | tf_op jit(solution)/shard_map/flash/pallas_call | solution.py:348
  112.9 0.1 collective-permute-start.9
  113.0 80.8 %flash.7 = bf16[136,1280]{1,0:T(8,128)(2,1)S(1)} custom-call(s32[2]{0:T(128)S(1)} %pad_add_fusion.me_ref, s32[4]{0:T(128)S(1)} %copy-done.1, bf16[80,2176]{1,0:T(8,128)(2,1)S(1)} %collective-permute-done.7.pq_ref, bf16[4608,256]{1,0:T(8,128)(2,1)S(1)} %get-tuple-element.48.k_ref, bf16[144,4608]{1,0:T(8,128)(2,1)S(1)} %get-tuple-element.49.vt_ref), custom_call_target="tpu_custom_call" | custom-call | flops 1 | bytes 1 | tf_op jit(solution)/shard_map/flash/pallas_call | solution.py:348
  193.8 0.1 collective-permute-start.10
  193.9 80.8 %flash.8 = bf16[136,1280]{1,0:T(8,128)(2,1)S(1)} custom-call(s32[2]{0:T(128)S(1)} %pad_add_fusion.me_ref, s32[4]{0:T(128)S(1)} %copy-done.1, bf16[80,2176]{1,0:T(8,128)(2,1)S(1)} %collective-permute-done.8.pq_ref, bf16[4608,256]{1,0:T(8,128)(2,1)S(1)} %get-tuple-element.48.k_ref, bf16[144,4608]{1,0:T(8,128)(2,1)S(1)} %get-tuple-element.49.vt_ref), custom_call_target="tpu_custom_call" | custom-call | flops 1 | bytes 1 | tf_op jit(solution)/shard_map/flash/pallas_call | solution.py:348
  274.6 0.1 collective-permute-start.11
  274.7 64.2 %flash.9.refs_1_ = bf16[136,1024]{1,0:T(8,128)(2,1)S(1)} custom-call(s32[2]{0:T(128)S(1)} %pad_add_fusion.me_ref, s32[4]{0:T(128)S(1)} %copy-done.1, bf16[80,2176]{1,0:T(8,128)(2,1)S(1)} %get-tuple-element.54.pq_ref, bf16[4608,256]{1,0:T(8,128)(2,1)S(1)} %get-tuple-element.48.k_ref, bf16[144,4608]{1,0:T(8,128)(2,1)S(1)} %get-tuple-element.49.vt_ref), custom_call_target="tpu_custom_call" | custom-call | flops 1 | bytes 1 | tf_op jit(solution)/shard_map/flash/pallas_call | solution.py:348
  339.0 0.7 merge.1
  339.6 6.4 %collective-permute-start.12 = (bf16[40,1024]{1,0:T(8,128)(2,1)S(1)}, bf16[40,1024]{1,0:T(8,128)(2,1)S(1)}, u32[]{:S(2)}, u32[]{:S(2)}) collective-permute-start(bf16[40,1024]{1,0:T(8,128)(2,1)S(1)} %get-tuple-element.59), channel_id=1, source_target_pairs={{0,1},{1,0},{2,3},{3,2},{4,5},{5,4},{6,7},{7,6},{8,9},{9,8},{10,11... | collective-permute-start | bytes 245768 | tf_op jit(solution)/shard_map/ppermute | solution.py:298
  346.0 8.6 %collective-permute-start.13 = (bf16[40,1024]{1,0:T(8,128)(2,1)S(1)}, bf16[40,1024]{1,0:T(8,128)(2,1)S(1)}, u32[]{:S(2)}, u32[]{:S(2)}) collective-permute-start(bf16[40,1024]{1,0:T(8,128)(2,1)S(1)} %get-tuple-element.60), channel_id=1, source_target_pairs={{0,2},{1,3},{2,0},{3,1},{4,6},{5,7},{6,4},{7,5},{8,10},{9,11},{10,... | collective-permute-start | bytes 245768 | tf_op jit(solution)/shard_map/ppermute | solution.py:298
  354.7 3.3 collective-permute-done.13.refs_2_
  358.0 3.1 collective-permute-done.14.refs_3_
  361.1 0.9 unroute.1
  (18 shorter events, 0.1 us)
Async XLA Ops:
  0.0 2.2 copy-start.2
  0.0 2.2 copy-start
  3.2 8.4 %collective-permute-start = (bf16[1152,256]{1,0:T(8,128)(2,1)S(1)}, bf16[1152,256]{1,0:T(8,128)(2,1)S(1)}, u32[]{:S(2)}, u32[]{:S(2)}) collective-permute-start(bf16[1152,256]{1,0:T(8,128)(2,1)S(1)} %get-tuple-element.36.refs_0_), channel_id=1, source_target_pairs={{0,4},{4,0},{8,12},{12,8},{16,20},{20,16},{24,28},{28,24},{1,5},{5... | collective-permute-start | bytes 1769480 | tf_op jit(solution)/shard_map/ppermute | solution.py:298
  3.7 17.4 %collective-permute-start.4 = (bf16[1152,256]{1,0:T(8,128)(2,1)S(1)}, bf16[1152,256]{1,0:T(8,128)(2,1)S(1)}, u32[]{:S(2)}, u32[]{:S(2)}) collective-permute-start(bf16[1152,256]{1,0:T(8,128)(2,1)S(1)} %get-tuple-element.63), channel_id=1, source_target_pairs={{0,24},{4,28},{8,16},{12,20},{16,8},{20,12},{24,0},{28,4},{1,25},{... | collective-permute-start | bytes 1769480 | tf_op jit(solution)/shard_map/ppermute | solution.py:298
  7.2 4.7 %collective-permute-start.1 = (bf16[40,1152]{1,0:T(8,128)(2,1)S(1)}, bf16[40,1152]{1,0:T(8,128)(2,1)S(1)}, u32[]{:S(2)}, u32[]{:S(2)}) collective-permute-start(bf16[40,1152]{1,0:T(8,128)(2,1)S(1)} %get-tuple-element.40), channel_id=1, source_target_pairs={{0,1},{1,0},{2,3},{3,2},{4,5},{5,4},{6,7},{7,6},{8,9},{9,8},{10,11... | collective-permute-start | bytes 276488 | tf_op jit(solution)/shard_map/ppermute | solution.py:298
  8.8 10.2 %collective-permute-start.2 = (bf16[40,1152]{1,0:T(8,128)(2,1)S(1)}, bf16[40,1152]{1,0:T(8,128)(2,1)S(1)}, u32[]{:S(2)}, u32[]{:S(2)}) collective-permute-start(bf16[40,1152]{1,0:T(8,128)(2,1)S(1)} %get-tuple-element.41), channel_id=1, source_target_pairs={{0,2},{1,3},{2,0},{3,1},{4,6},{5,7},{6,4},{7,5},{8,10},{9,11},{10,... | collective-permute-start | bytes 276488 | tf_op jit(solution)/shard_map/ppermute | solution.py:298
  11.4 7.7 %collective-permute-start.3 = (bf16[40,1152]{1,0:T(8,128)(2,1)S(1)}, bf16[40,1152]{1,0:T(8,128)(2,1)S(1)}, u32[]{:S(2)}, u32[]{:S(2)}) collective-permute-start(bf16[40,1152]{1,0:T(8,128)(2,1)S(1)} %get-tuple-element.42), channel_id=1, source_target_pairs={{0,3},{1,2},{2,1},{3,0},{4,7},{5,6},{6,5},{7,4},{8,11},{9,10},{10,... | collective-permute-start | bytes 276488 | tf_op jit(solution)/shard_map/ppermute | solution.py:298
  21.2 3.8 %copy-start.1 = (s32[4]{0:T(128)S(1)}, s32[4]{0:T(128)}, u32[]{:S(2)}) copy-start(s32[4]{0:T(128)} %len_ref.9) | copy-start | bytes 52
  21.2 3.5 collective-permute-start.5
  21.2 10.9 %collective-permute-start.6 = (bf16[80,2176]{1,0:T(8,128)(2,1)S(1)}, bf16[80,2176]{1,0:T(8,128)(2,1)S(1)}, u32[]{:S(2)}, u32[]{:S(2)}) collective-permute-start(bf16[80,2176]{1,0:T(8,128)(2,1)S(1)} %get-tuple-element.54.pq_ref), channel_id=1, source_target_pairs={{0,8},{4,12},{8,0},{12,4},{16,24},{20,28},{24,16},{28,20},{1,9},{5... | collective-permute-start | bytes 1044488 | tf_op jit(solution)/shard_map/ppermute | solution.py:298
  22.9 90.1 %collective-permute-start.7 = (bf16[80,2176]{1,0:T(8,128)(2,1)S(1)}, bf16[80,2176]{1,0:T(8,128)(2,1)S(1)}, u32[]{:S(2)}, u32[]{:S(2)}) collective-permute-start(bf16[80,2176]{1,0:T(8,128)(2,1)S(1)} %get-tuple-element.54.pq_ref), channel_id=1, source_target_pairs={{0,16},{4,20},{8,24},{12,28},{16,0},{20,4},{24,8},{28,12},{1,17},{... | collective-permute-start | bytes 1044488 | tf_op jit(solution)/shard_map/ppermute | solution.py:298
  24.4 169.5 %collective-permute-start.8 = (bf16[80,2176]{1,0:T(8,128)(2,1)S(1)}, bf16[80,2176]{1,0:T(8,128)(2,1)S(1)}, u32[]{:S(2)}, u32[]{:S(2)}) collective-permute-start(bf16[80,2176]{1,0:T(8,128)(2,1)S(1)} %get-tuple-element.54.pq_ref), channel_id=1, source_target_pairs={{0,24},{4,28},{8,16},{12,20},{16,8},{20,12},{24,0},{28,4},{1,25},{... | collective-permute-start | bytes 1044488 | tf_op jit(solution)/shard_map/ppermute | solution.py:298
  112.9 161.7 %collective-permute-start.9 = (bf16[136,1280]{1,0:T(8,128)(2,1)S(1)}, bf16[136,1280]{1,0:T(8,128)(2,1)S(1)}, u32[]{:S(2)}, u32[]{:S(2)}) collective-permute-start(bf16[136,1280]{1,0:T(8,128)(2,1)S(1)} %flash.6), channel_id=1, source_target_pairs={{0,8},{4,12},{8,0},{12,4},{16,24},{20,28},{24,16},{28,20},{1,9},{5... | collective-permute-start | bytes 1044488 | tf_op jit(solution)/shard_map/ppermute | solution.py:298
  193.8 80.9 %collective-permute-start.10 = (bf16[136,1280]{1,0:T(8,128)(2,1)S(1)}, bf16[136,1280]{1,0:T(8,128)(2,1)S(1)}, u32[]{:S(2)}, u32[]{:S(2)}) collective-permute-start(bf16[136,1280]{1,0:T(8,128)(2,1)S(1)} %flash.7), channel_id=1, source_target_pairs={{0,16},{4,20},{8,24},{12,28},{16,0},{20,4},{24,8},{28,12},{1,17},{... | collective-permute-start | bytes 1044488 | tf_op jit(solution)/shard_map/ppermute | solution.py:298
  274.6 64.3 %collective-permute-start.11 = (bf16[136,1280]{1,0:T(8,128)(2,1)S(1)}, bf16[136,1280]{1,0:T(8,128)(2,1)S(1)}, u32[]{:S(2)}, u32[]{:S(2)}) collective-permute-start(bf16[136,1280]{1,0:T(8,128)(2,1)S(1)} %flash.8), channel_id=1, source_target_pairs={{0,24},{4,28},{8,16},{12,20},{16,8},{20,12},{24,0},{28,4},{1,25},{... | collective-permute-start | bytes 1044488 | tf_op jit(solution)/shard_map/ppermute | solution.py:298
  339.6 15.1 %collective-permute-start.12 = (bf16[40,1024]{1,0:T(8,128)(2,1)S(1)}, bf16[40,1024]{1,0:T(8,128)(2,1)S(1)}, u32[]{:S(2)}, u32[]{:S(2)}) collective-permute-start(bf16[40,1024]{1,0:T(8,128)(2,1)S(1)} %get-tuple-element.59), channel_id=1, source_target_pairs={{0,1},{1,0},{2,3},{3,2},{4,5},{5,4},{6,7},{7,6},{8,9},{9,8},{10,11... | collective-permute-start | bytes 245768 | tf_op jit(solution)/shard_map/ppermute | solution.py:298
  346.0 11.9 %collective-permute-start.13 = (bf16[40,1024]{1,0:T(8,128)(2,1)S(1)}, bf16[40,1024]{1,0:T(8,128)(2,1)S(1)}, u32[]{:S(2)}, u32[]{:S(2)}) collective-permute-start(bf16[40,1024]{1,0:T(8,128)(2,1)S(1)} %get-tuple-element.60), channel_id=1, source_target_pairs={{0,2},{1,3},{2,0},{3,1},{4,6},{5,7},{6,4},{7,5},{8,10},{9,11},{10,... | collective-permute-start | bytes 245768 | tf_op jit(solution)/shard_map/ppermute | solution.py:298
  354.7 6.4 %collective-permute-start.14 = (bf16[40,1024]{1,0:T(8,128)(2,1)S(1)}, bf16[40,1024]{1,0:T(8,128)(2,1)S(1)}, u32[]{:S(2)}, u32[]{:S(2)}) collective-permute-start(bf16[40,1024]{1,0:T(8,128)(2,1)S(1)} %get-tuple-element.61), channel_id=1, source_target_pairs={{0,3},{1,2},{2,1},{3,0},{4,7},{5,6},{6,5},{7,4},{8,11},{9,10},{10,... | collective-permute-start | bytes 245768 | tf_op jit(solution)/shard_map/ppermute | solution.py:298
where the time goes:
time: 364 us; the launch traced here: 362 us
  Pallas kernels  313 us (86%)
  starting transfers between devices  27.2 us (7%)
  waiting for transfers between devices  19.5 us (5%)
    pallas_call x5, Pallas kernels, flash(): call(functools.partial(flash_kernel, first, chips, half), bf(OUT_ROWS, ti...  309 us
    ppermute x15, starting transfers between devices, swapped(): return lax.ppermute(block, axis, [(i, i ^ distance) for i in devices])  27.2 us
    ppermute x15, waiting for transfers between devices, swapped(): return lax.ppermute(block, axis, [(i, i ^ distance) for i in devices])  19.5 us
  transfers between devices with their start and end apart: 15, of which 5 were waited for; matrix products, arithmetic and copies ran while one was open for 0% of the time, Pallas kernels for 86%

commit v1 on v0

--- a/solution.py
+++ b/solution.py
@@ -27,6 +27,10 @@
     return lax.dot_general(a, b, dims, preferred_element_type=jnp.float32)
 
 
+def in_hbm(x):
+    return pltpu.with_memory_space_constraint(x, pltpu.HBM)
+
+
 def iota(shape, dim):
     return lax.broadcasted_iota(jnp.int32, shape, dim)
 
@@ -35,7 +39,7 @@
     return jnp.transpose(jnp.broadcast_to(column, (column.shape[0], 128)), (1, 0))[:1, :]
 
 
-def call(body, out_shape, in_specs, name, scratch=(), limit=48, aliases=None):
+def call(body, out_shape, in_specs, name, scratch=(), limit=20, aliases=None):
     many = isinstance(out_shape, list)
     return pl.pallas_call(
         body,
@@ -57,15 +61,24 @@
     return fold
 
 
-def route_kernel(capacity, me_ref, req_ref, pos_ref, q_ref, *outs):
+def route_kernel(capacity, me_ref, req_hbm, pos_hbm, q_hbm, *outs):
+    outs, (req_ref, pos_ref, q_ref, sem) = outs[:-4], outs[-4:]
     sends, back_ref = outs[:-1], outs[-1]
+    fetches = [
+        pltpu.make_async_copy(src, dst, sem.at[i])
+        for i, (src, dst) in enumerate(((req_hbm, req_ref), (pos_hbm, pos_ref), (q_hbm, q_ref)))
+    ]
+    for fetch in fetches:
+        fetch.start()
+    for fetch in fetches:
+        fetch.wait()
     rows = q_ref.shape[0]
     fold = fold_of(capacity)
     block, width = capacity * fold, WIDE // fold
-    target_c = req_ref[...]
-    target_r = row_of(target_c.astype(jnp.float32)).astype(jnp.int32)
+    i0, i1 = iota((rows, rows), 0), iota((rows, rows), 1)
+    target_r = req_ref[...]
+    target_c = jnp.sum(jnp.where(i0 == i1, target_r, 0), axis=1, keepdims=True)
     same = target_c == target_r
-    i0, i1 = iota((rows, rows), 0), iota((rows, rows), 1)
     rank_c = jnp.sum((same & (i1 < i0)).astype(jnp.int32), axis=1, keepdims=True)
     rank_r = jnp.sum((same & (i0 < i1)).astype(jnp.int32), axis=0, keepdims=True)
     slot_c = (target_c ^ me_ref[1]) * block + rank_c
@@ -128,17 +141,21 @@
         back_ref[f] = ((rank_c == iota((total, slots), 1)) & (part_c == f)).astype(jnp.bfloat16)
 
 
-def keys_kernel(first, count, *refs):
-    pieces, k_ref, vt_ref = refs[:count], refs[-2], refs[-1]
-    piece = pieces[0].shape[0]
-    extra = vt_ref.shape[0] - HD
-    ones = (iota((extra, piece), 0) == 0).astype(jnp.bfloat16)
-    for i, ref in enumerate(pieces, first):
-        at = slice(i * piece, (i + 1) * piece)
-        k_ref[at, :HD] = ref[:, :HD]
-        k_ref[at, HD:] = ref[:, :HD]
-        vt_ref[:HD, at] = jnp.transpose(ref[:, HD:], (1, 0))
-        vt_ref[HD:, at] = ones
+def store_keys(k_ref, vt_ref, number, piece):
+    count = piece.shape[0]
+    at = slice(number * count, (number + 1) * count)
+    k_ref[at, :HD] = piece[:, :HD]
+    k_ref[at, HD:] = piece[:, :HD]
+    vt_ref[:HD, at] = jnp.transpose(piece[:, HD:], (1, 0))
+    vt_ref[HD:, at] = (iota((vt_ref.shape[0] - HD, count), 0) == 0).astype(jnp.bfloat16)
+
+
+def keys_kernel(first, pieces, *refs):
+    k_ref, vt_ref = refs[-2:]
+    at = 0
+    for number, count in enumerate(pieces, first):
+        store_keys(k_ref, vt_ref, number, jnp.concatenate([ref[...] for ref in refs[at : at + count]], axis=0))
+        at += count
 
 
 def flash_kernel(
@@ -150,11 +167,12 @@
     pieces, pairs = 4, 2
     length = len_ref[me_ref[1]]
     chip, core = me_ref[0] // 2, lax.rem(me_ref[0], 2)
-    kept_at, away_at = chip * (4 * piece), (chips - 1 - chip) * (4 * piece) + piece
-    rising = kept_at < away_at
+    home_at = chip * (4 * piece)
+    away_at = (chips - 1 - chip) * (4 * piece) + piece
+    rising = home_at < away_at
     for pair, kept in enumerate((rising, jnp.logical_not(rising))):
         for k in range(2):
-            info_ref[2 * pair + k] = jnp.where(kept, kept_at, away_at) + 2 * piece * k
+            info_ref[2 * pair + k] = jnp.where(kept, home_at, away_at) + 2 * piece * k
             info_ref[pieces + 2 * pair + k] = jnp.where(kept, 0, 2) + jnp.where(core == k, 0, 1)
     meta = pq_ref[first * TILE : (first + tiles) * TILE, WIDE:].astype(jnp.float32)
     pos = meta[:, 0:1] * 256.0 + meta[:, 1:2] - 1.0
@@ -314,20 +332,26 @@
     me = jnp.stack([here, mine]).astype(jnp.int32)
     bf = lambda *shape: jax.ShapeDtypeStruct(shape, jnp.bfloat16)
 
-    other = cycle - 2
-    away = swapped(cache[0, half:], "ctx", other)
+    away = swapped(cache[0, half:], "ctx", cycle - 2)
 
     *sends, back_tok = call(
         functools.partial(route_kernel, capacity),
         [bf(block, width + META)] * groups + [bf(fold, tok_rows, groups * block)],
-        [SMEM] + [VMEM] * 3,
+        [SMEM] + [pl.BlockSpec(memory_space=pltpu.HBM)] * 3,
         "route",
-    )(me, req_of, q_pos.reshape(1, tok_rows), queries)
-    sends[0], kept = lax.optimization_barrier((sends[0], cache[0, :half]))
-    blocks = [sends[0]] + [swapped(sends[d], "req", d) for d in range(1, groups)]
+        scratch=[
+            pltpu.VMEM((1, tok_rows), jnp.int32),
+            pltpu.VMEM((1, tok_rows), jnp.int32),
+            pltpu.VMEM((tok_rows, WIDE), jnp.bfloat16),
+            pltpu.SemaphoreType.DMA((3,)),
+        ],
+    )(me, *[in_hbm(x) for x in (req_of.reshape(1, tok_rows), q_pos.reshape(1, tok_rows), queries)])
+    blocks = {d: swapped(sends[d], "req", d) for d in reversed(range(1, groups))}
+    blocks[0], span = lax.optimization_barrier((sends[0], cache[0]))
+    kept = span[:half]
     kept_sib = swapped(kept, "ctx", 1)
     all_keys = [bf(4 * half, 2 * HD), bf(HD + 16, 4 * half)]
-    kept_keys = call(functools.partial(keys_kernel, 0, 2), all_keys, [VMEM] * 2, "keys_kept")(kept, kept_sib)
+    kept_keys = call(functools.partial(keys_kernel, 0, (1, 1)), all_keys, [VMEM] * 2, "kept_keys")(kept, kept_sib)
     blocks[0], *kept_keys = lax.optimization_barrier((blocks[0], *kept_keys))
 
     sorted_q, back_slot = call(
@@ -335,13 +359,14 @@
         [bf(slots, WIDE + META), bf(fold, groups * block, slots)],
         [VMEM] * groups,
         "sort",
-    )(*blocks)
+    )(*[blocks[d] for d in range(groups)])
     visiting = {d: swapped(sorted_q, "ctx", 2 * d) for d in range(1, chips)}
     sorted_q, away = lax.optimization_barrier((sorted_q, away))
-    away_sib = swapped(away, "ctx", 1)
+    away_sib = [swapped(away[i * half // 2 : (i + 1) * half // 2], "ctx", 1) for i in range(2)]
+
     k_all, vt_all = call(
-        functools.partial(keys_kernel, 2, 2), all_keys, [VMEM] * 4, "keys_away", aliases={2: 0, 3: 1}
-    )(away, away_sib, *kept_keys)
+        functools.partial(keys_kernel, 2, (1, 2)), all_keys, [VMEM] * 5, "away_keys", aliases={3: 0, 4: 1}
+    )(away, *away_sib, *kept_keys)
 
     def flash(q, first=0, tiles=slots // TILE):
         extra = (tiles + 1) * TILE * H
@@ -361,7 +386,7 @@
             ],
         )(me, cache_len, q, k_all, vt_all)
 
-    turn = flash(sorted_q, 0, 1)
+    turn = flash(sorted_q, 0, 2)
     own = [turn]
     home = []
     for d in sorted(visiting, key=lambda d: (d & (d - 1) != 0, d)):
@@ -371,7 +396,7 @@
             turn, *home = lax.optimization_barrier((turn, *home))
         home.append(swapped(turn, "ctx", 2 * d))
     turn, q = lax.optimization_barrier((turn, sorted_q))
-    own.append(flash(q, 1, slots // TILE - 1))
+    own.append(flash(q, 2, slots // TILE - 2))
     home = [*own, *home]
     outs = call(
         functools.partial(merge_kernel, len(home) - 2),

time: 364 us -> 366 us (level); the launches traced: 362 us -> 369 us
  starting transfers between devices: 27.2 us -> 51.1 us
  Pallas kernels: 313 us -> 299 us
    ppermute x15 -> x16, starting transfers between devices: 27.2 us -> 51.1 us  [swapped(): return lax.ppermute(block, axis, [(i, i ^ distance) for i in devices])]
    pallas_call x5, Pallas kernels: 309 us -> 295 us  [flash(): call(functools.partial(flash_kernel, first, chips, half), bf(OUT_ROWS, ti...]
    ppermute x15 -> x16, waiting for transfers between devices: 19.5 us -> 16.8 us  [swapped(): return lax.ppermute(block, axis, [(i, i ^ distance) for i in devices])]
  transfers between devices with their start and end apart: 15 -> 16, of which waited for: 5 -> 6; matrix products, arithmetic and copies ran while one was open for 0% -> 0% of each run, Pallas kernels for 86% -> 80%
where the time goes in v1:
time: 366 us; the launch traced here: 369 us
  Pallas kernels  299 us (82%)
  starting transfers between devices  51.1 us (14%)
  waiting for transfers between devices  16.8 us (5%)
    pallas_call x5, Pallas kernels, flash(): call(functools.partial(flash_kernel, first, chips, half), bf(OUT_ROWS, ti...  295 us
    ppermute x16, starting transfers between devices, swapped(): return lax.ppermute(block, axis, [(i, i ^ distance) for i in devices])  51.1 us
    ppermute x16, waiting for transfers between devices, swapped(): return lax.ppermute(block, axis, [(i, i ^ distance) for i in devices])  16.8 us
  transfers between devices with their start and end apart: 16, of which 6 were waited for; matrix products, arithmetic and copies ran while one was open for 0% of the time, Pallas kernels for 80%

profile of v1, /device:TPU:0, one launch (start us, length us, event | category | flops | bytes accessed | tf_op | source)
XLA Modules:
  0.0 368.6 jit_solution(8928784561086265312)
XLA Ops:
  0.0 0.1 pad_add_fusion.me_ref
  0.1 2.0 route.1
  2.1 1.1 slice.12.refs_0_
  3.2 0.5 collective-permute-start
  3.7 3.5 collective-permute-start.4
  7.3 1.6 collective-permute-start.1
  8.8 2.6 collective-permute-start.2
  11.4 0.2 collective-permute-start.3
  11.7 0.3 kept_keys.1
  12.0 7.0 %collective-permute-done.2.refs_2_ = bf16[40,1152]{1,0:T(8,128)(2,1)S(1)} collective-permute-done((bf16[40,1152]{1,0:T(8,128)(2,1)S(1)}, bf16[40,1152]{1,0:T(8,128)(2,1)S(1)}, u32[]{:S(2)}, u32[]{:S(2)}) %collective-permute-start.2) | collective-permute-done | bytes 92192 | tf_op jit(solution)/shard_map/ppermute | solution.py:316
  19.1 0.5 sort.1
  19.6 0.6 collective-permute-start.7
  20.2 0.5 collective-permute-start.8
  20.7 0.7 collective-permute-done.4.refs_0_
  21.5 0.1 collective-permute-start.5
  21.6 0.5 collective-permute-start.6
  22.1 2.8 collective-permute-start.9
  24.9 0.3 away_keys.1
  25.2 2.8 flash.5.refs_0_
  28.1 2.7 collective-permute-done.7.pq_ref
  30.8 80.8 %flash.6 = bf16[136,1280]{1,0:T(8,128)(2,1)S(1)} custom-call(s32[2]{0:T(128)S(1)} %pad_add_fusion.me_ref, s32[4]{0:T(128)S(1)} %copy-done, bf16[80,2176]{1,0:T(8,128)(2,1)S(1)} %collective-permute-done.7.pq_ref, bf16[4608,256]{1,0:T(8,128)(2,1)S(1)} %get-tuple-element.48.k_ref, bf16[144,4608]{1,0:T(8,128)(2,1)S(1)} %get-tuple-element.49.vt_ref), custom_call_target="tpu_custom_call" | custom-call | flops 1 | bytes 1 | tf_op jit(solution)/shard_map/flash/pallas_call | solution.py:373
  111.6 0.1 collective-permute-start.10
  111.6 80.8 %flash.7 = bf16[136,1280]{1,0:T(8,128)(2,1)S(1)} custom-call(s32[2]{0:T(128)S(1)} %pad_add_fusion.me_ref, s32[4]{0:T(128)S(1)} %copy-done, bf16[80,2176]{1,0:T(8,128)(2,1)S(1)} %collective-permute-done.8.pq_ref, bf16[4608,256]{1,0:T(8,128)(2,1)S(1)} %get-tuple-element.48.k_ref, bf16[144,4608]{1,0:T(8,128)(2,1)S(1)} %get-tuple-element.49.vt_ref), custom_call_target="tpu_custom_call" | custom-call | flops 1 | bytes 1 | tf_op jit(solution)/shard_map/flash/pallas_call | solution.py:373
  192.5 80.8 %flash.8 = bf16[136,1280]{1,0:T(8,128)(2,1)S(1)} custom-call(s32[2]{0:T(128)S(1)} %pad_add_fusion.me_ref, s32[4]{0:T(128)S(1)} %copy-done, bf16[80,2176]{1,0:T(8,128)(2,1)S(1)} %collective-permute-done.9.pq_ref, bf16[4608,256]{1,0:T(8,128)(2,1)S(1)} %get-tuple-element.48.k_ref, bf16[144,4608]{1,0:T(8,128)(2,1)S(1)} %get-tuple-element.49.vt_ref), custom_call_target="tpu_custom_call" | custom-call | flops 1 | bytes 1 | tf_op jit(solution)/shard_map/flash/pallas_call | solution.py:373
  273.3 0.1 collective-permute-start.12
  273.4 49.4 %flash.9.refs_1_ = bf16[136,768]{1,0:T(8,128)(2,1)S(1)} custom-call(s32[2]{0:T(128)S(1)} %pad_add_fusion.me_ref, s32[4]{0:T(128)S(1)} %copy-done, bf16[80,2176]{1,0:T(8,128)(2,1)S(1)} %get-tuple-element.54.pq_ref, bf16[4608,256]{1,0:T(8,128)(2,1)S(1)} %get-tuple-element.48.k_ref, bf16[144,4608]{1,0:T(8,128)(2,1)S(1)} %get-tuple-element.49.vt_ref), custom_call_target="tpu_custom_call" | custom-call | flops 1 | bytes 1 | tf_op jit(solution)/shard_map/flash/pallas_call | solution.py:373
  322.8 0.7 merge.1
  323.5 0.1 collective-permute-start.13
  323.6 37.9 %collective-permute-start.14 = (bf16[40,1024]{1,0:T(8,128)(2,1)S(1)}, bf16[40,1024]{1,0:T(8,128)(2,1)S(1)}, u32[]{:S(2)}, u32[]{:S(2)}) collective-permute-start(bf16[40,1024]{1,0:T(8,128)(2,1)S(1)} %get-tuple-element.60), channel_id=1, source_target_pairs={{0,2},{1,3},{2,0},{3,1},{4,6},{5,7},{6,4},{7,5},{8,10},{9,11},{10,... | collective-permute-start | bytes 245768 | tf_op jit(solution)/shard_map/ppermute | solution.py:316
  361.4 3.3 collective-permute-done.14.refs_2_
  364.7 2.9 collective-permute-done.15.refs_3_
  367.7 0.9 unroute.1
  (19 shorter events, 0.3 us)
Async XLA Ops:
  0.0 3.7 copy-start.1
  3.2 8.5 %collective-permute-start = (bf16[1152,256]{1,0:T(8,128)(2,1)S(1)}, bf16[1152,256]{1,0:T(8,128)(2,1)S(1)}, u32[]{:S(2)}, u32[]{:S(2)}) collective-permute-start(bf16[1152,256]{1,0:T(8,128)(2,1)S(1)} %slice.12.refs_0_), channel_id=1, source_target_pairs={{0,4},{4,0},{8,12},{12,8},{16,20},{20,16},{24,28},{28,24},{1,5},{5... | collective-permute-start | bytes 1769480 | tf_op jit(solution)/shard_map/ppermute | solution.py:316
  3.7 17.7 %collective-permute-start.4 = (bf16[1152,256]{1,0:T(8,128)(2,1)S(1)}, bf16[1152,256]{1,0:T(8,128)(2,1)S(1)}, u32[]{:S(2)}, u32[]{:S(2)}) collective-permute-start(bf16[1152,256]{1,0:T(8,128)(2,1)S(1)} %slice_bitcast_fusion), channel_id=1, source_target_pairs={{0,24},{4,28},{8,16},{12,20},{16,8},{20,12},{24,0},{28,4},{1,25},{... | collective-permute-start | bytes 1769480 | tf_op jit(solution)/shard_map/ppermute | solution.py:316
  7.3 4.8 %collective-permute-start.1 = (bf16[40,1152]{1,0:T(8,128)(2,1)S(1)}, bf16[40,1152]{1,0:T(8,128)(2,1)S(1)}, u32[]{:S(2)}, u32[]{:S(2)}) collective-permute-start(bf16[40,1152]{1,0:T(8,128)(2,1)S(1)} %get-tuple-element.40), channel_id=1, source_target_pairs={{0,1},{1,0},{2,3},{3,2},{4,5},{5,4},{6,7},{7,6},{8,9},{9,8},{10,11... | collective-permute-start | bytes 276488 | tf_op jit(solution)/shard_map/ppermute | solution.py:316
  8.8 10.2 %collective-permute-start.2 = (bf16[40,1152]{1,0:T(8,128)(2,1)S(1)}, bf16[40,1152]{1,0:T(8,128)(2,1)S(1)}, u32[]{:S(2)}, u32[]{:S(2)}) collective-permute-start(bf16[40,1152]{1,0:T(8,128)(2,1)S(1)} %get-tuple-element.41), channel_id=1, source_target_pairs={{0,2},{1,3},{2,0},{3,1},{4,6},{5,7},{6,4},{7,5},{8,10},{9,11},{10,... | collective-permute-start | bytes 276488 | tf_op jit(solution)/shard_map/ppermute | solution.py:316
  11.4 7.7 %collective-permute-start.3 = (bf16[40,1152]{1,0:T(8,128)(2,1)S(1)}, bf16[40,1152]{1,0:T(8,128)(2,1)S(1)}, u32[]{:S(2)}, u32[]{:S(2)}) collective-permute-start(bf16[40,1152]{1,0:T(8,128)(2,1)S(1)} %get-tuple-element.42), channel_id=1, source_target_pairs={{0,3},{1,2},{2,1},{3,0},{4,7},{5,6},{6,5},{7,4},{8,11},{9,10},{10,... | collective-permute-start | bytes 276488 | tf_op jit(solution)/shard_map/ppermute | solution.py:316
  19.6 11.2 %collective-permute-start.7 = (bf16[80,2176]{1,0:T(8,128)(2,1)S(1)}, bf16[80,2176]{1,0:T(8,128)(2,1)S(1)}, u32[]{:S(2)}, u32[]{:S(2)}) collective-permute-start(bf16[80,2176]{1,0:T(8,128)(2,1)S(1)} %get-tuple-element.54.pq_ref), channel_id=1, source_target_pairs={{0,8},{4,12},{8,0},{12,4},{16,24},{20,28},{24,16},{28,20},{1,9},{5... | collective-permute-start | bytes 1044488 | tf_op jit(solution)/shard_map/ppermute | solution.py:316
  20.2 91.4 %collective-permute-start.8 = (bf16[80,2176]{1,0:T(8,128)(2,1)S(1)}, bf16[80,2176]{1,0:T(8,128)(2,1)S(1)}, u32[]{:S(2)}, u32[]{:S(2)}) collective-permute-start(bf16[80,2176]{1,0:T(8,128)(2,1)S(1)} %get-tuple-element.54.pq_ref), channel_id=1, source_target_pairs={{0,16},{4,20},{8,24},{12,28},{16,0},{20,4},{24,8},{28,12},{1,17},{... | collective-permute-start | bytes 1044488 | tf_op jit(solution)/shard_map/ppermute | solution.py:316
  21.5 3.4 collective-permute-start.5
  21.6 3.7 copy-start
  21.6 3.3 collective-permute-start.6
  22.1 170.4 %collective-permute-start.9 = (bf16[80,2176]{1,0:T(8,128)(2,1)S(1)}, bf16[80,2176]{1,0:T(8,128)(2,1)S(1)}, u32[]{:S(2)}, u32[]{:S(2)}) collective-permute-start(bf16[80,2176]{1,0:T(8,128)(2,1)S(1)} %get-tuple-element.54.pq_ref), channel_id=1, source_target_pairs={{0,24},{4,28},{8,16},{12,20},{16,8},{20,12},{24,0},{28,4},{1,25},{... | collective-permute-start | bytes 1044488 | tf_op jit(solution)/shard_map/ppermute | solution.py:316
  111.6 161.8 %collective-permute-start.10 = (bf16[136,1280]{1,0:T(8,128)(2,1)S(1)}, bf16[136,1280]{1,0:T(8,128)(2,1)S(1)}, u32[]{:S(2)}, u32[]{:S(2)}) collective-permute-start(bf16[136,1280]{1,0:T(8,128)(2,1)S(1)} %flash.6), channel_id=1, source_target_pairs={{0,8},{4,12},{8,0},{12,4},{16,24},{20,28},{24,16},{28,20},{1,9},{5... | collective-permute-start | bytes 1044488 | tf_op jit(solution)/shard_map/ppermute | solution.py:316
  192.4 80.9 %collective-permute-start.11 = (bf16[136,1280]{1,0:T(8,128)(2,1)S(1)}, bf16[136,1280]{1,0:T(8,128)(2,1)S(1)}, u32[]{:S(2)}, u32[]{:S(2)}) collective-permute-start(bf16[136,1280]{1,0:T(8,128)(2,1)S(1)} %flash.7), channel_id=1, source_target_pairs={{0,16},{4,20},{8,24},{12,28},{16,0},{20,4},{24,8},{28,12},{1,17},{... | collective-permute-start | bytes 1044488 | tf_op jit(solution)/shard_map/ppermute | solution.py:316
  273.3 49.5 %collective-permute-start.12 = (bf16[136,1280]{1,0:T(8,128)(2,1)S(1)}, bf16[136,1280]{1,0:T(8,128)(2,1)S(1)}, u32[]{:S(2)}, u32[]{:S(2)}) collective-permute-start(bf16[136,1280]{1,0:T(8,128)(2,1)S(1)} %flash.8), channel_id=1, source_target_pairs={{0,24},{4,28},{8,16},{12,20},{16,8},{20,12},{24,0},{28,4},{1,25},{... | collective-permute-start | bytes 1044488 | tf_op jit(solution)/shard_map/ppermute | solution.py:316
  323.5 38.0 %collective-permute-start.13 = (bf16[40,1024]{1,0:T(8,128)(2,1)S(1)}, bf16[40,1024]{1,0:T(8,128)(2,1)S(1)}, u32[]{:S(2)}, u32[]{:S(2)}) collective-permute-start(bf16[40,1024]{1,0:T(8,128)(2,1)S(1)} %get-tuple-element.59), channel_id=1, source_target_pairs={{0,1},{1,0},{2,3},{3,2},{4,5},{5,4},{6,7},{7,6},{8,9},{9,8},{10,11... | collective-permute-start | bytes 245768 | tf_op jit(solution)/shard_map/ppermute | solution.py:316
  323.6 41.2 %collective-permute-start.14 = (bf16[40,1024]{1,0:T(8,128)(2,1)S(1)}, bf16[40,1024]{1,0:T(8,128)(2,1)S(1)}, u32[]{:S(2)}, u32[]{:S(2)}) collective-permute-start(bf16[40,1024]{1,0:T(8,128)(2,1)S(1)} %get-tuple-element.60), channel_id=1, source_target_pairs={{0,2},{1,3},{2,0},{3,1},{4,6},{5,7},{6,4},{7,5},{8,10},{9,11},{10,... | collective-permute-start | bytes 245768 | tf_op jit(solution)/shard_map/ppermute | solution.py:316
  361.4 6.2 %collective-permute-start.15 = (bf16[40,1024]{1,0:T(8,128)(2,1)S(1)}, bf16[40,1024]{1,0:T(8,128)(2,1)S(1)}, u32[]{:S(2)}, u32[]{:S(2)}) collective-permute-start(bf16[40,1024]{1,0:T(8,128)(2,1)S(1)} %get-tuple-element.61), channel_id=1, source_target_pairs={{0,3},{1,2},{2,1},{3,0},{4,7},{5,6},{6,5},{7,4},{8,11},{9,10},{10,... | collective-permute-start | bytes 245768 | tf_op jit(solution)/shard_map/ppermute | solution.py:316

commit v2 on v1

--- a/solution.py
+++ b/solution.py
@@ -61,16 +61,16 @@
     return fold
 
 
-def route_kernel(capacity, me_ref, req_hbm, pos_hbm, q_hbm, *outs):
+def route_kernel(capacity, me_ref, req_hbm, pos_hbm, q_hbm, shard_hbm, *outs):
     outs, (req_ref, pos_ref, q_ref, sem) = outs[:-4], outs[-4:]
-    sends, back_ref = outs[:-1], outs[-1]
-    fetches = [
-        pltpu.make_async_copy(src, dst, sem.at[i])
-        for i, (src, dst) in enumerate(((req_hbm, req_ref), (pos_hbm, pos_ref), (q_hbm, q_ref)))
-    ]
+    sends, back_ref, halves = outs[:-3], outs[-3], outs[-2:]
+    half = halves[0].shape[0]
+    moves = [(req_hbm, req_ref), (pos_hbm, pos_ref), (q_hbm, q_ref)]
+    moves += [(shard_hbm.at[pl.ds(i * half, half)], halves[i]) for i in range(2)]
+    fetches = [pltpu.make_async_copy(src, dst, sem.at[i]) for i, (src, dst) in enumerate(moves)]
     for fetch in fetches:
         fetch.start()
-    for fetch in fetches:
+    for fetch in fetches[:3]:
         fetch.wait()
     rows = q_ref.shape[0]
     fold = fold_of(capacity)
@@ -100,6 +100,8 @@
     for d, out in enumerate(sends):
         out[:, :width] = moved[d * block : (d + 1) * block]
         out[:, width:] = meta[d * block : (d + 1) * block]
+    for fetch in fetches[3:]:
+        fetch.wait()
 
 
 def row_parts(shape, dim, capacity):
@@ -121,7 +123,7 @@
     slots = out.shape[0]
     fold = fold_of(capacity)
     width = WIDE // fold
-    joined = jnp.concatenate([b[...] for b in blocks], axis=0)
+    joined = jnp.concatenate([b[...] for b in reversed(blocks)], axis=0)
     total = joined.shape[0]
     meta = joined[:, width:].astype(jnp.float32)
     pos_c = meta[:, 0:1] * 256.0 + meta[:, 1:2]
@@ -306,7 +308,7 @@
 def unroute_kernel(*refs):
     blocks, back_ref, out = refs[:-2], refs[-2], refs[-1]
     width = blocks[0].shape[1]
-    joined = jnp.concatenate([b[...] for b in blocks], axis=0)
+    joined = jnp.concatenate([b[...] for b in reversed(blocks)], axis=0)
     for f in range(back_ref.shape[0]):
         out[:, f * width : (f + 1) * width] = dot(back_ref[f], joined).astype(jnp.bfloat16)
 
@@ -332,23 +334,21 @@
     me = jnp.stack([here, mine]).astype(jnp.int32)
     bf = lambda *shape: jax.ShapeDtypeStruct(shape, jnp.bfloat16)
 
-    away = swapped(cache[0, half:], "ctx", cycle - 2)
-
-    *sends, back_tok = call(
+    *sends, back_tok, kept, away = call(
         functools.partial(route_kernel, capacity),
-        [bf(block, width + META)] * groups + [bf(fold, tok_rows, groups * block)],
-        [SMEM] + [pl.BlockSpec(memory_space=pltpu.HBM)] * 3,
+        [bf(block, width + META)] * groups + [bf(fold, tok_rows, groups * block)] + [bf(half, 2 * HD)] * 2,
+        [SMEM] + [pl.BlockSpec(memory_space=pltpu.HBM)] * 4,
         "route",
         scratch=[
             pltpu.VMEM((1, tok_rows), jnp.int32),
             pltpu.VMEM((1, tok_rows), jnp.int32),
             pltpu.VMEM((tok_rows, WIDE), jnp.bfloat16),
-            pltpu.SemaphoreType.DMA((3,)),
+            pltpu.SemaphoreType.DMA((5,)),
         ],
-    )(me, *[in_hbm(x) for x in (req_of.reshape(1, tok_rows), q_pos.reshape(1, tok_rows), queries)])
+    )(me, *[in_hbm(x) for x in (req_of.reshape(1, tok_rows), q_pos.reshape(1, tok_rows), queries, cache[0])])
     blocks = {d: swapped(sends[d], "req", d) for d in reversed(range(1, groups))}
-    blocks[0], span = lax.optimization_barrier((sends[0], cache[0]))
-    kept = span[:half]
+    blocks[0] = sends[0]
+    away = swapped(away, "ctx", cycle - 2)
     kept_sib = swapped(kept, "ctx", 1)
     all_keys = [bf(4 * half, 2 * HD), bf(HD + 16, 4 * half)]
     kept_keys = call(functools.partial(keys_kernel, 0, (1, 1)), all_keys, [VMEM] * 2, "kept_keys")(kept, kept_sib)
@@ -359,7 +359,7 @@
         [bf(slots, WIDE + META), bf(fold, groups * block, slots)],
         [VMEM] * groups,
         "sort",
-    )(*[blocks[d] for d in range(groups)])
+    )(*[blocks[d] for d in reversed(range(groups))])
     visiting = {d: swapped(sorted_q, "ctx", 2 * d) for d in range(1, chips)}
     sorted_q, away = lax.optimization_barrier((sorted_q, away))
     away_sib = [swapped(away[i * half // 2 : (i + 1) * half // 2], "ctx", 1) for i in range(2)]
@@ -392,10 +392,8 @@
     for d in sorted(visiting, key=lambda d: (d & (d - 1) != 0, d)):
         turn, q = lax.optimization_barrier((turn, visiting[d]))
         turn = flash(q)
-        if d == chips - 1:
-            turn, *home = lax.optimization_barrier((turn, *home))
         home.append(swapped(turn, "ctx", 2 * d))
-    turn, q = lax.optimization_barrier((turn, sorted_q))
+    turn, q, *home[:-1] = lax.optimization_barrier((turn, sorted_q, *home[:-1]))
     own.append(flash(q, 2, slots // TILE - 2))
     home = [*own, *home]
     outs = call(
@@ -405,7 +403,7 @@
         "merge",
         scratch=[pltpu.VMEM((slots, WIDE), jnp.bfloat16)],
     )(*home, back_slot)
-    back = [outs[0]] + [swapped(outs[d], "req", d) for d in range(1, groups)]
+    back = [swapped(outs[d], "req", d) for d in reversed(range(1, groups))] + [outs[0]]
     return call(unroute_kernel, bf(tok_rows, WIDE), [VMEM] * (groups + 1), "unroute")(*back, back_tok)
 
 

time: 366 us -> 360 us (0.984)
  Pallas kernels: 299 us -> 225 us
  starting transfers between devices: 51.1 us -> 111 us
  waiting for transfers between devices: 16.8 us -> 23.5 us
    pallas_call x5, Pallas kernels: 295 us -> 220 us  [flash(): call(functools.partial(flash_kernel, first, chips, half), bf(OUT_ROWS, ti...]
    ppermute x16, starting transfers between devices: 51.1 us -> 111 us  [swapped(): return lax.ppermute(block, axis, [(i, i ^ distance) for i in devices])]
    ppermute x16, waiting for transfers between devices: 16.8 us -> 23.5 us  [swapped(): return lax.ppermute(block, axis, [(i, i ^ distance) for i in devices])]
  transfers between devices with their start and end apart: 16 -> 16, of which waited for: 6 -> 8; matrix products, arithmetic and copies ran while one was open for 0% -> 0% of each run, Pallas kernels for 80% -> 61%
where the time goes in v2:
time: 360 us; the launch traced here: 359 us
  Pallas kernels  225 us (62%)
  starting transfers between devices  111 us (31%)
  waiting for transfers between devices  23.5 us (7%)
    pallas_call x5, Pallas kernels, flash(): call(functools.partial(flash_kernel, first, chips, half), bf(OUT_ROWS, ti...  220 us
    ppermute x16, starting transfers between devices, swapped(): return lax.ppermute(block, axis, [(i, i ^ distance) for i in devices])  111 us
    ppermute x16, waiting for transfers between devices, swapped(): return lax.ppermute(block, axis, [(i, i ^ distance) for i in devices])  23.5 us
  transfers between devices with their start and end apart: 16, of which 8 were waited for; matrix products, arithmetic and copies ran while one was open for 0% of the time, Pallas kernels for 61%

profile of v2, /device:TPU:0, one launch (start us, length us, event | category | flops | bytes accessed | tf_op | source)
XLA Modules:
  0.0 359.5 jit_solution(3632978589912566367)
XLA Ops:
  0.0 0.1 pad_add_fusion.me_ref
  0.1 2.0 route.1
  2.1 0.5 collective-permute-start.3
  2.6 3.5 collective-permute-start.4
  6.1 3.6 %collective-permute-start = (bf16[40,1152]{1,0:T(8,128)(2,1)S(1)}, bf16[40,1152]{1,0:T(8,128)(2,1)S(1)}, u32[]{:S(2)}, u32[]{:S(2)}) collective-permute-start(bf16[40,1152]{1,0:T(8,128)(2,1)S(1)} %get-tuple-element.33), channel_id=1, source_target_pairs={{0,3},{1,2},{2,1},{3,0},{4,7},{5,6},{6,5},{7,4},{8,11},{9,10},{10,... | collective-permute-start | bytes 276488 | tf_op jit(solution)/shard_map/ppermute | solution.py:318
  9.7 0.8 collective-permute-start.2
  10.5 0.3 kept_keys.1
  10.8 2.7 collective-permute-done.refs_0_
  13.5 4.3 %collective-permute-done.1.refs_1_ = bf16[40,1152]{1,0:T(8,128)(2,1)S(1)} collective-permute-done((bf16[40,1152]{1,0:T(8,128)(2,1)S(1)}, bf16[40,1152]{1,0:T(8,128)(2,1)S(1)}, u32[]{:S(2)}, u32[]{:S(2)}) %collective-permute-start.1) | collective-permute-done | bytes 92192 | tf_op jit(solution)/shard_map/ppermute | solution.py:318
  17.8 0.5 sort.1
  18.3 0.6 collective-permute-start.7
  18.9 0.5 collective-permute-start.8
  19.4 2.5 collective-permute-start.9
  22.0 0.5 collective-permute-start.6
  22.5 1.1 collective-permute-done.5.refs_1_
  23.6 0.4 collective-permute-done.6.refs_2_
  24.0 0.3 away_keys.1
  24.3 2.8 flash.5.refs_0_
  27.2 2.3 collective-permute-done.7.pq_ref
  29.5 80.8 %flash.6 = bf16[136,1280]{1,0:T(8,128)(2,1)S(1)} custom-call(s32[2]{0:T(128)S(1)} %pad_add_fusion.me_ref, s32[4]{0:T(128)S(1)} %copy-done, bf16[80,2176]{1,0:T(8,128)(2,1)S(1)} %collective-permute-done.7.pq_ref, bf16[4608,256]{1,0:T(8,128)(2,1)S(1)} %get-tuple-element.47.k_ref, bf16[144,4608]{1,0:T(8,128)(2,1)S(1)} %get-tuple-element.48.vt_ref), custom_call_target="tpu_custom_call" | custom-call | flops 1 | bytes 1 | tf_op jit(solution)/shard_map/flash/pallas_call | solution.py:373
  110.3 0.1 collective-permute-start.10
  110.4 80.8 %flash.7 = bf16[136,1280]{1,0:T(8,128)(2,1)S(1)} custom-call(s32[2]{0:T(128)S(1)} %pad_add_fusion.me_ref, s32[4]{0:T(128)S(1)} %copy-done, bf16[80,2176]{1,0:T(8,128)(2,1)S(1)} %collective-permute-done.8.pq_ref, bf16[4608,256]{1,0:T(8,128)(2,1)S(1)} %get-tuple-element.47.k_ref, bf16[144,4608]{1,0:T(8,128)(2,1)S(1)} %get-tuple-element.48.vt_ref), custom_call_target="tpu_custom_call" | custom-call | flops 1 | bytes 1 | tf_op jit(solution)/shard_map/flash/pallas_call | solution.py:373
  191.2 0.1 collective-permute-start.11
  191.2 6.0 %flash.8 = bf16[136,1280]{1,0:T(8,128)(2,1)S(1)} custom-call(s32[2]{0:T(128)S(1)} %pad_add_fusion.me_ref, s32[4]{0:T(128)S(1)} %copy-done, bf16[80,2176]{1,0:T(8,128)(2,1)S(1)} %collective-permute-done.9.pq_ref, bf16[4608,256]{1,0:T(8,128)(2,1)S(1)} %get-tuple-element.47.k_ref, bf16[144,4608]{1,0:T(8,128)(2,1)S(1)} %get-tuple-element.48.vt_ref), custom_call_target="tpu_custom_call" | custom-call | flops 1 | bytes 1 | tf_op jit(solution)/shard_map/flash/pallas_call | solution.py:373
  197.3 7.1 %collective-permute-done.11.refs_3_ = bf16[136,1280]{1,0:T(8,128)(2,1)S(1)} collective-permute-done((bf16[136,1280]{1,0:T(8,128)(2,1)S(1)}, bf16[136,1280]{1,0:T(8,128)(2,1)S(1)}, u32[]{:S(2)}, u32[]{:S(2)}) %collective-permute-start.11) | collective-permute-done | bytes 348192 | tf_op jit(solution)/shard_map/ppermute | solution.py:318
  204.4 49.4 %flash.9.refs_1_ = bf16[136,768]{1,0:T(8,128)(2,1)S(1)} custom-call(s32[2]{0:T(128)S(1)} %pad_add_fusion.me_ref, s32[4]{0:T(128)S(1)} %copy-done, bf16[80,2176]{1,0:T(8,128)(2,1)S(1)} %get-tuple-element.52.pq_ref, bf16[4608,256]{1,0:T(8,128)(2,1)S(1)} %get-tuple-element.47.k_ref, bf16[144,4608]{1,0:T(8,128)(2,1)S(1)} %get-tuple-element.48.vt_ref), custom_call_target="tpu_custom_call" | custom-call | flops 1 | bytes 1 | tf_op jit(solution)/shard_map/flash/pallas_call | solution.py:373
  253.8 0.7 merge.1
  254.5 97.8 %collective-permute-start.13 = (bf16[40,1024]{1,0:T(8,128)(2,1)S(1)}, bf16[40,1024]{1,0:T(8,128)(2,1)S(1)}, u32[]{:S(2)}, u32[]{:S(2)}) collective-permute-start(bf16[40,1024]{1,0:T(8,128)(2,1)S(1)} %get-tuple-element.56), channel_id=1, source_target_pairs={{0,3},{1,2},{2,1},{3,0},{4,7},{5,6},{6,5},{7,4},{8,11},{9,10},{10,... | collective-permute-start | bytes 245768 | tf_op jit(solution)/shard_map/ppermute | solution.py:318
  352.3 0.6 collective-permute-start.15
  352.9 2.0 collective-permute-done.13.refs_0_
  354.9 3.6 %collective-permute-done.14.refs_1_ = bf16[40,1024]{1,0:T(8,128)(2,1)S(1)} collective-permute-done((bf16[40,1024]{1,0:T(8,128)(2,1)S(1)}, bf16[40,1024]{1,0:T(8,128)(2,1)S(1)}, u32[]{:S(2)}, u32[]{:S(2)}) %collective-permute-start.14) | collective-permute-done | bytes 81952 | tf_op jit(solution)/shard_map/ppermute | solution.py:318
  358.5 0.9 unroute.1
  (15 shorter events, 0.2 us)
Async XLA Ops:
  2.1 8.4 %collective-permute-start.3 = (bf16[1152,256]{1,0:T(8,128)(2,1)S(1)}, bf16[1152,256]{1,0:T(8,128)(2,1)S(1)}, u32[]{:S(2)}, u32[]{:S(2)}) collective-permute-start(bf16[1152,256]{1,0:T(8,128)(2,1)S(1)} %get-tuple-element.37.refs_0_), channel_id=1, source_target_pairs={{0,4},{4,0},{8,12},{12,8},{16,20},{20,16},{24,28},{28,24},{1,5},{5... | collective-permute-start | bytes 1769480 | tf_op jit(solution)/shard_map/ppermute | solution.py:318
  2.6 19.3 %collective-permute-start.4 = (bf16[1152,256]{1,0:T(8,128)(2,1)S(1)}, bf16[1152,256]{1,0:T(8,128)(2,1)S(1)}, u32[]{:S(2)}, u32[]{:S(2)}) collective-permute-start(bf16[1152,256]{1,0:T(8,128)(2,1)S(1)} %get-tuple-element.42), channel_id=1, source_target_pairs={{0,24},{4,28},{8,16},{12,20},{16,8},{20,12},{24,0},{28,4},{1,25},{... | collective-permute-start | bytes 1769480 | tf_op jit(solution)/shard_map/ppermute | solution.py:318
  6.1 7.4 %collective-permute-start = (bf16[40,1152]{1,0:T(8,128)(2,1)S(1)}, bf16[40,1152]{1,0:T(8,128)(2,1)S(1)}, u32[]{:S(2)}, u32[]{:S(2)}) collective-permute-start(bf16[40,1152]{1,0:T(8,128)(2,1)S(1)} %get-tuple-element.33), channel_id=1, source_target_pairs={{0,3},{1,2},{2,1},{3,0},{4,7},{5,6},{6,5},{7,4},{8,11},{9,10},{10,... | collective-permute-start | bytes 276488 | tf_op jit(solution)/shard_map/ppermute | solution.py:318
  9.7 8.1 %collective-permute-start.1 = (bf16[40,1152]{1,0:T(8,128)(2,1)S(1)}, bf16[40,1152]{1,0:T(8,128)(2,1)S(1)}, u32[]{:S(2)}, u32[]{:S(2)}) collective-permute-start(bf16[40,1152]{1,0:T(8,128)(2,1)S(1)} %get-tuple-element.34), channel_id=1, source_target_pairs={{0,2},{1,3},{2,0},{3,1},{4,6},{5,7},{6,4},{7,5},{8,10},{9,11},{10,... | collective-permute-start | bytes 276488 | tf_op jit(solution)/shard_map/ppermute | solution.py:318
  9.7 8.1 %collective-permute-start.2 = (bf16[40,1152]{1,0:T(8,128)(2,1)S(1)}, bf16[40,1152]{1,0:T(8,128)(2,1)S(1)}, u32[]{:S(2)}, u32[]{:S(2)}) collective-permute-start(bf16[40,1152]{1,0:T(8,128)(2,1)S(1)} %get-tuple-element.35), channel_id=1, source_target_pairs={{0,1},{1,0},{2,3},{3,2},{4,5},{5,4},{6,7},{7,6},{8,9},{9,8},{10,11... | collective-permute-start | bytes 276488 | tf_op jit(solution)/shard_map/ppermute | solution.py:318
  18.3 11.2 %collective-permute-start.7 = (bf16[80,2176]{1,0:T(8,128)(2,1)S(1)}, bf16[80,2176]{1,0:T(8,128)(2,1)S(1)}, u32[]{:S(2)}, u32[]{:S(2)}) collective-permute-start(bf16[80,2176]{1,0:T(8,128)(2,1)S(1)} %get-tuple-element.52.pq_ref), channel_id=1, source_target_pairs={{0,8},{4,12},{8,0},{12,4},{16,24},{20,28},{24,16},{28,20},{1,9},{5... | collective-permute-start | bytes 1044488 | tf_op jit(solution)/shard_map/ppermute | solution.py:318
  18.9 91.4 %collective-permute-start.8 = (bf16[80,2176]{1,0:T(8,128)(2,1)S(1)}, bf16[80,2176]{1,0:T(8,128)(2,1)S(1)}, u32[]{:S(2)}, u32[]{:S(2)}) collective-permute-start(bf16[80,2176]{1,0:T(8,128)(2,1)S(1)} %get-tuple-element.52.pq_ref), channel_id=1, source_target_pairs={{0,16},{4,20},{8,24},{12,28},{16,0},{20,4},{24,8},{28,12},{1,17},{... | collective-permute-start | bytes 1044488 | tf_op jit(solution)/shard_map/ppermute | solution.py:318
  19.4 171.8 %collective-permute-start.9 = (bf16[80,2176]{1,0:T(8,128)(2,1)S(1)}, bf16[80,2176]{1,0:T(8,128)(2,1)S(1)}, u32[]{:S(2)}, u32[]{:S(2)}) collective-permute-start(bf16[80,2176]{1,0:T(8,128)(2,1)S(1)} %get-tuple-element.52.pq_ref), channel_id=1, source_target_pairs={{0,24},{4,28},{8,16},{12,20},{16,8},{20,12},{24,0},{28,4},{1,25},{... | collective-permute-start | bytes 1044488 | tf_op jit(solution)/shard_map/ppermute | solution.py:318
  21.9 1.6 collective-permute-start.5
  22.0 2.3 copy-start
  22.0 2.0 collective-permute-start.6
  110.3 87.0 %collective-permute-start.10 = (bf16[136,1280]{1,0:T(8,128)(2,1)S(1)}, bf16[136,1280]{1,0:T(8,128)(2,1)S(1)}, u32[]{:S(2)}, u32[]{:S(2)}) collective-permute-start(bf16[136,1280]{1,0:T(8,128)(2,1)S(1)} %flash.6), channel_id=1, source_target_pairs={{0,8},{4,12},{8,0},{12,4},{16,24},{20,28},{24,16},{28,20},{1,9},{5... | collective-permute-start | bytes 1044488 | tf_op jit(solution)/shard_map/ppermute | solution.py:318
  191.2 13.3 %collective-permute-start.11 = (bf16[136,1280]{1,0:T(8,128)(2,1)S(1)}, bf16[136,1280]{1,0:T(8,128)(2,1)S(1)}, u32[]{:S(2)}, u32[]{:S(2)}) collective-permute-start(bf16[136,1280]{1,0:T(8,128)(2,1)S(1)} %flash.7), channel_id=1, source_target_pairs={{0,16},{4,20},{8,24},{12,28},{16,0},{20,4},{24,8},{28,12},{1,17},{... | collective-permute-start | bytes 1044488 | tf_op jit(solution)/shard_map/ppermute | solution.py:318
  197.2 56.6 %collective-permute-start.12 = (bf16[136,1280]{1,0:T(8,128)(2,1)S(1)}, bf16[136,1280]{1,0:T(8,128)(2,1)S(1)}, u32[]{:S(2)}, u32[]{:S(2)}) collective-permute-start(bf16[136,1280]{1,0:T(8,128)(2,1)S(1)} %flash.8), channel_id=1, source_target_pairs={{0,24},{4,28},{8,16},{12,20},{16,8},{20,12},{24,0},{28,4},{1,25},{... | collective-permute-start | bytes 1044488 | tf_op jit(solution)/shard_map/ppermute | solution.py:318
  254.5 100.4 %collective-permute-start.13 = (bf16[40,1024]{1,0:T(8,128)(2,1)S(1)}, bf16[40,1024]{1,0:T(8,128)(2,1)S(1)}, u32[]{:S(2)}, u32[]{:S(2)}) collective-permute-start(bf16[40,1024]{1,0:T(8,128)(2,1)S(1)} %get-tuple-element.56), channel_id=1, source_target_pairs={{0,3},{1,2},{2,1},{3,0},{4,7},{5,6},{6,5},{7,4},{8,11},{9,10},{10,... | collective-permute-start | bytes 245768 | tf_op jit(solution)/shard_map/ppermute | solution.py:318
  352.3 6.2 %collective-permute-start.14 = (bf16[40,1024]{1,0:T(8,128)(2,1)S(1)}, bf16[40,1024]{1,0:T(8,128)(2,1)S(1)}, u32[]{:S(2)}, u32[]{:S(2)}) collective-permute-start(bf16[40,1024]{1,0:T(8,128)(2,1)S(1)} %get-tuple-element.57), channel_id=1, source_target_pairs={{0,2},{1,3},{2,0},{3,1},{4,6},{5,7},{6,4},{7,5},{8,10},{9,11},{10,... | collective-permute-start | bytes 245768 | tf_op jit(solution)/shard_map/ppermute | solution.py:318
  352.3 6.2 %collective-permute-start.15 = (bf16[40,1024]{1,0:T(8,128)(2,1)S(1)}, bf16[40,1024]{1,0:T(8,128)(2,1)S(1)}, u32[]{:S(2)}, u32[]{:S(2)}) collective-permute-start(bf16[40,1024]{1,0:T(8,128)(2,1)S(1)} %get-tuple-element.58), channel_id=1, source_target_pairs={{0,1},{1,0},{2,3},{3,2},{4,5},{5,4},{6,7},{7,6},{8,9},{9,8},{10,11... | collective-permute-start | bytes 245768 | tf_op jit(solution)/shard_map/ppermute | solution.py:318

commit v3 on v2

--- a/solution.py
+++ b/solution.py
@@ -166,7 +166,7 @@
     width = TILE * H
     all_width = out_ref.shape[1]
     tiles = all_width // width
-    pieces, pairs = 4, 2
+    pieces = 4
     length = len_ref[me_ref[1]]
     chip, core = me_ref[0] // 2, lax.rem(me_ref[0], 2)
     home_at = chip * (4 * piece)
@@ -179,13 +179,11 @@
     meta = pq_ref[first * TILE : (first + tiles) * TILE, WIDE:].astype(jnp.float32)
     pos = meta[:, 0:1] * 256.0 + meta[:, 1:2] - 1.0
     last = jnp.minimum(pos, (length - 1).astype(jnp.float32))
-    count = jnp.int32(0)
+    tops, lows = [], []
     for j in range(tiles):
         here = last[j * TILE : (j + 1) * TILE]
-        top = jnp.max(here).astype(jnp.int32)
-        for i in range(pairs):
-            job_ref[count] = j * pairs + i
-            count += (info_ref[2 * i] <= top).astype(jnp.int32)
+        tops.append(jnp.max(here).astype(jnp.int32))
+        lows.append(jnp.min(here).astype(jnp.int32))
         row_ref[0:1, j * width : (j + 1) * width] = jnp.concatenate([row_of(here)] * H, axis=1)
         rows = slice((first + j) * TILE, (first + j + 1) * TILE)
         for h in range(H):
@@ -194,15 +192,26 @@
             at = slice(j * width + h * TILE, j * width + (h + 1) * TILE)
             q_ref[at, :HD] = high
             q_ref[at, HD:] = (x - high.astype(jnp.float32)).astype(jnp.bfloat16)
+    count, whole = jnp.int32(0), []
+    for j in range(tiles):
+        for i in range(pieces):
+            whole.append(info_ref[i] + (piece - 1) <= lows[j])
+            job_ref[count] = j * pieces + i
+            count += whole[-1].astype(jnp.int32)
+    whole_turns = count // 2
+    for j in range(tiles):
+        for i in range(pieces):
+            job_ref[count] = j * pieces + i
+            count += ((info_ref[i] <= tops[j]) & jnp.logical_not(whole[j * pieces + i])).astype(jnp.int32)
     for k in range(3):
-        job_ref[count + k] = tiles * pairs
+        job_ref[count + k] = tiles * pieces
     row_ref[0:1, all_width:] = jnp.full((1, width), -1.0, jnp.float32)
     q_ref[all_width:, :] = jnp.zeros((width, 2 * HD), jnp.bfloat16)
     acc_ref[...] = jnp.zeros_like(acc_ref)
 
     def place(job):
-        tile = job // pairs
-        return pl.ds(pl.multiple_of(tile * width, width), width), 2 * (job - tile * pairs)
+        tile = job // pieces
+        return pl.ds(pl.multiple_of(tile * width, width), width), job - tile * pieces
 
     def keys(c, a, n):
         return pl.ds(pl.multiple_of(info_ref[pieces + c] * piece + a, 128), n)
@@ -222,30 +231,28 @@
             cols, c = place(job_ref[k])
             s_ref[k] = scores(cols, c, *subs[0])
 
-    def turn(b, carry):
+    def turn(b, mask):
         now = [place(job_ref[2 * b + k]) for k in range(2)]
         later = [place(job_ref[2 * b + 2 + k]) for k in range(2)]
-        steps = [(g, a, n) for g in range(2) for a, n in subs]
         s = [s_ref[k] for k in range(2)]
         totals = [None, None]
-        for i, (g, a, n) in enumerate(steps):
-            if i + 1 < len(steps):
-                g2, a2, n2 = steps[i + 1]
-                next_s = [scores(cols, c + g2, a2, n2) for cols, c in now]
+        for i, (a, n) in enumerate(subs):
+            if i + 1 < len(subs):
+                next_s = [scores(cols, c, *subs[i + 1]) for cols, c in now]
             else:
                 next_s = [scores(cols, c, *subs[0]) for cols, c in later]
             for k, (cols, c) in enumerate(now):
-                weights = jnp.exp2(masked(s[k], cols, c + g, a)).astype(jnp.bfloat16)
-                term = dot(vt_ref[:, keys(c + g, a, n)], weights)
+                weights = jnp.exp2(masked(s[k], cols, c, a) if mask else s[k]).astype(jnp.bfloat16)
+                term = dot(vt_ref[:, keys(c, a, n)], weights)
                 totals[k] = term if totals[k] is None else totals[k] + term
             s = next_s
         for k in range(2):
             s_ref[k] = s[k]
         for k, (cols, _) in enumerate(now):
             acc_ref[:, cols] += totals[k]
-        return carry
-
-    lax.fori_loop(0, (count + 1) // 2, turn, 0)
+
+    pl.loop(0, whole_turns)(lambda b: turn(b, False))
+    pl.loop(whole_turns, (count + 1) // 2)(lambda b: turn(b, True))
     top_ref[0:1, :] = jnp.zeros((1, all_width), jnp.float32)
     total = acc_ref[HD : HD + 1, :all_width]
     dead = row_ref[0:1, :all_width] < info_ref[0].astype(jnp.float32)
@@ -282,14 +289,17 @@
     out_ref[HD:, :] = terms.astype(jnp.bfloat16)
 
 
-def merge_kernel(count, *refs):
-    own, parts, back_ref, outs, slot_ref = refs[:2], refs[2 : count + 2], refs[count + 2], refs[count + 3 : -1], refs[-1]
+def merge_kernel(cuts, *refs):
+    count = sum(cuts)
+    pieces, back_ref, outs, slot_ref = list(refs[:count]), refs[count], refs[count + 1 : -1], refs[-1]
     fold = back_ref.shape[0]
     width = TILE * H
-    split = own[0].shape[1] // width
+    parts = []
+    for cut in cuts:
+        taken, pieces = pieces[:cut], pieces[cut:]
+        parts.append([(ref, slice(i, i + width)) for ref in taken for i in range(0, ref.shape[1], width)])
     for j in range(slot_ref.shape[0] // TILE):
-        here = [(own[0], j) if j < split else (own[1], j - split)] + [(part, j) for part in parts]
-        here = [(part, slice(i * width, (i + 1) * width)) for part, i in here]
+        here = [part[j] for part in parts]
         lses = [sum(part[HD + i : HD + i + 1, cols].astype(jnp.float32) for i in range(3)) for part, cols in here]
         high = functools.reduce(jnp.maximum, lses)
         shares = [jnp.exp2(lse - high) for lse in lses]
@@ -381,23 +391,29 @@
                 pltpu.VMEM((8, extra), jnp.float32),
                 pltpu.VMEM((2, SUB, TILE * H), jnp.float32),
                 pltpu.VMEM((8, tiles * TILE * H), jnp.float32),
-                pltpu.SMEM((2 * tiles + 4,), jnp.int32),
+                pltpu.SMEM((4 * tiles + 4,), jnp.int32),
                 pltpu.SMEM((8,), jnp.int32),
             ],
         )(me, cache_len, q, k_all, vt_all)
 
+    tiles = slots // TILE
+    last = max(visiting, key=lambda d: (d & (d - 1) != 0, d))
     turn = flash(sorted_q, 0, 2)
-    own = [turn]
-    home = []
-    for d in sorted(visiting, key=lambda d: (d & (d - 1) != 0, d)):
-        turn, q = lax.optimization_barrier((turn, visiting[d]))
-        turn = flash(q)
-        home.append(swapped(turn, "ctx", 2 * d))
-    turn, q, *home[:-1] = lax.optimization_barrier((turn, sorted_q, *home[:-1]))
-    own.append(flash(q, 2, slots // TILE - 2))
-    home = [*own, *home]
+    own, home = [turn], {}
+    for d in sorted(visiting, key=lambda d: (d == last, d & (d - 1) != 0, d)):
+        home[d] = []
+        for at, count in ((0, 3), (3, tiles - 3)) if d == last else ((0, tiles),):
+            turn, q = lax.optimization_barrier((turn, visiting[d]))
+            turn = flash(q, at, count)
+            home[d].append(swapped(turn, "ctx", 2 * d))
+    before = [home[d][0] for d in home if d != last]
+    turn, q, *before = lax.optimization_barrier((turn, sorted_q, *before))
+    own.append(flash(q, 2, tiles - 2))
+    home = [own, home[last], *[[part] for part in before]]
+    cuts = tuple(len(part) for part in home)
+    home = [ref for part in home for ref in part]
     outs = call(
-        functools.partial(merge_kernel, len(home) - 2),
+        functools.partial(merge_kernel, cuts),
         [bf(block, width)] * groups,
         [VMEM] * (len(home) + 1),
         "merge",

time: 360 us -> 360 us (level)
  starting transfers between devices: 111 us -> 122 us
  waiting for transfers between devices: 23.5 us -> 15.8 us
  Pallas kernels: 225 us -> 220 us
    ppermute x16 -> x17, starting transfers between devices: 111 us -> 122 us  [swapped(): return lax.ppermute(block, axis, [(i, i ^ distance) for i in devices])]
    ppermute x16 -> x17, waiting for transfers between devices: 23.5 us -> 15.8 us  [swapped(): return lax.ppermute(block, axis, [(i, i ^ distance) for i in devices])]
    pallas_call x5 -> x6, Pallas kernels: 220 us -> 215 us  [flash(): call(functools.partial(flash_kernel, first, chips, half), bf(OUT_ROWS, ti...]
  transfers between devices with their start and end apart: 16 -> 17, of which waited for: 8 -> 7; matrix products, arithmetic and copies ran while one was open for 0% -> 0% of each run, Pallas kernels for 61% -> 60%
where the time goes in v3:
time: 360 us; the launch traced here: 358 us
  Pallas kernels  220 us (61%)
  starting transfers between devices  122 us (34%)
  waiting for transfers between devices  15.8 us (4%)
    pallas_call x6, Pallas kernels, flash(): call(functools.partial(flash_kernel, first, chips, half), bf(OUT_ROWS, ti...  215 us
    ppermute x17, starting transfers between devices, swapped(): return lax.ppermute(block, axis, [(i, i ^ distance) for i in devices])  122 us
    ppermute x17, waiting for transfers between devices, swapped(): return lax.ppermute(block, axis, [(i, i ^ distance) for i in devices])  15.8 us
  transfers between devices with their start and end apart: 17, of which 7 were waited for; matrix products, arithmetic and copies ran while one was open for 0% of the time, Pallas kernels for 60%

profile of v3, /device:TPU:0, one launch (start us, length us, event | category | flops | bytes accessed | tf_op | source)
XLA Modules:
  0.0 358.4 jit_solution(3962396537770778884)
XLA Ops:
  0.0 0.1 pad_add_fusion.me_ref
  0.1 2.0 route.1
  2.1 0.5 collective-permute-start.3
  2.6 3.5 collective-permute-start.4
  6.1 3.6 %collective-permute-start = (bf16[40,1152]{1,0:T(8,128)(2,1)S(1)}, bf16[40,1152]{1,0:T(8,128)(2,1)S(1)}, u32[]{:S(2)}, u32[]{:S(2)}) collective-permute-start(bf16[40,1152]{1,0:T(8,128)(2,1)S(1)} %get-tuple-element.34), channel_id=1, source_target_pairs={{0,3},{1,2},{2,1},{3,0},{4,7},{5,6},{6,5},{7,4},{8,11},{9,10},{10,... | collective-permute-start | bytes 276488 | tf_op jit(solution)/shard_map/ppermute | solution.py:328
  9.7 0.8 collective-permute-start.2
  10.5 0.3 kept_keys.1
  10.8 2.7 collective-permute-done.refs_0_
  13.5 4.3 %collective-permute-done.1.refs_1_ = bf16[40,1152]{1,0:T(8,128)(2,1)S(1)} collective-permute-done((bf16[40,1152]{1,0:T(8,128)(2,1)S(1)}, bf16[40,1152]{1,0:T(8,128)(2,1)S(1)}, u32[]{:S(2)}, u32[]{:S(2)}) %collective-permute-start.1) | collective-permute-done | bytes 92192 | tf_op jit(solution)/shard_map/ppermute | solution.py:328
  17.8 0.5 sort.1
  18.3 0.6 collective-permute-start.7
  18.9 0.5 collective-permute-start.8
  19.4 0.6 collective-permute-done.4.refs_0_
  20.2 0.5 collective-permute-start.6
  20.7 3.1 collective-permute-start.9
  23.8 0.3 away_keys.1
  24.1 3.7 %flash.6.refs_0_ = bf16[136,512]{1,0:T(8,128)(2,1)S(1)} custom-call(s32[2]{0:T(128)S(1)} %pad_add_fusion.me_ref, s32[4]{0:T(128)S(1)} %copy-done, bf16[80,2176]{1,0:T(8,128)(2,1)S(1)} %get-tuple-element.54.pq_ref, bf16[4608,256]{1,0:T(8,128)(2,1)S(1)} %get-tuple-element.48.k_ref, bf16[144,4608]{1,0:T(8,128)(2,1)S(1)} %get-tuple-element.49.vt_ref), custom_call_target="tpu_custom_call" | custom-call | flops 1 | bytes 1 | tf_op jit(solution)/shard_map/flash/pallas_call | solution.py:383
  27.8 1.7 collective-permute-done.7.pq_ref
  29.5 79.5 %flash.7 = bf16[136,1280]{1,0:T(8,128)(2,1)S(1)} custom-call(s32[2]{0:T(128)S(1)} %pad_add_fusion.me_ref, s32[4]{0:T(128)S(1)} %copy-done, bf16[80,2176]{1,0:T(8,128)(2,1)S(1)} %collective-permute-done.7.pq_ref, bf16[4608,256]{1,0:T(8,128)(2,1)S(1)} %get-tuple-element.48.k_ref, bf16[144,4608]{1,0:T(8,128)(2,1)S(1)} %get-tuple-element.49.vt_ref), custom_call_target="tpu_custom_call" | custom-call | flops 1 | bytes 1 | tf_op jit(solution)/shard_map/flash/pallas_call | solution.py:383
  109.0 0.1 collective-permute-start.10
  109.1 79.5 %flash.8 = bf16[136,1280]{1,0:T(8,128)(2,1)S(1)} custom-call(s32[2]{0:T(128)S(1)} %pad_add_fusion.me_ref, s32[4]{0:T(128)S(1)} %copy-done, bf16[80,2176]{1,0:T(8,128)(2,1)S(1)} %collective-permute-done.8.pq_ref, bf16[4608,256]{1,0:T(8,128)(2,1)S(1)} %get-tuple-element.48.k_ref, bf16[144,4608]{1,0:T(8,128)(2,1)S(1)} %get-tuple-element.49.vt_ref), custom_call_target="tpu_custom_call" | custom-call | flops 1 | bytes 1 | tf_op jit(solution)/shard_map/flash/pallas_call | solution.py:383
  188.6 49.3 %flash.9 = bf16[136,768]{1,0:T(8,128)(2,1)S(1)} custom-call(s32[2]{0:T(128)S(1)} %pad_add_fusion.me_ref, s32[4]{0:T(128)S(1)} %copy-done, bf16[80,2176]{1,0:T(8,128)(2,1)S(1)} %collective-permute-done.9.pq_ref, bf16[4608,256]{1,0:T(8,128)(2,1)S(1)} %get-tuple-element.48.k_ref, bf16[144,4608]{1,0:T(8,128)(2,1)S(1)} %get-tuple-element.49.vt_ref), custom_call_target="tpu_custom_call" | custom-call | flops 1 | bytes 1 | tf_op jit(solution)/shard_map/flash/pallas_call | solution.py:383
  238.1 1.2 flash.10
  239.3 3.0 collective-permute-start.13
  242.2 2.1 flash.11.refs_1_
  244.4 1.8 collective-permute-done.13.refs_3_
  246.2 0.7 merge.1
  246.9 105.2 %collective-permute-start.14 = (bf16[40,1024]{1,0:T(8,128)(2,1)S(1)}, bf16[40,1024]{1,0:T(8,128)(2,1)S(1)}, u32[]{:S(2)}, u32[]{:S(2)}) collective-permute-start(bf16[40,1024]{1,0:T(8,128)(2,1)S(1)} %get-tuple-element.58), channel_id=1, source_target_pairs={{0,3},{1,2},{2,1},{3,0},{4,7},{5,6},{6,5},{7,4},{8,11},{9,10},{10,... | collective-permute-start | bytes 245768 | tf_op jit(solution)/shard_map/ppermute | solution.py:328
  352.1 0.6 collective-permute-start.16
  352.7 1.8 collective-permute-done.14.refs_0_
  354.5 2.9 collective-permute-done.15.refs_1_
  357.4 0.9 unroute.1
  (18 shorter events, 0.3 us)
Async XLA Ops:
  2.1 8.4 %collective-permute-start.3 = (bf16[1152,256]{1,0:T(8,128)(2,1)S(1)}, bf16[1152,256]{1,0:T(8,128)(2,1)S(1)}, u32[]{:S(2)}, u32[]{:S(2)}) collective-permute-start(bf16[1152,256]{1,0:T(8,128)(2,1)S(1)} %get-tuple-element.38.refs_0_), channel_id=1, source_target_pairs={{0,4},{4,0},{8,12},{12,8},{16,20},{20,16},{24,28},{28,24},{1,5},{5... | collective-permute-start | bytes 1769480 | tf_op jit(solution)/shard_map/ppermute | solution.py:328
  2.6 17.4 %collective-permute-start.4 = (bf16[1152,256]{1,0:T(8,128)(2,1)S(1)}, bf16[1152,256]{1,0:T(8,128)(2,1)S(1)}, u32[]{:S(2)}, u32[]{:S(2)}) collective-permute-start(bf16[1152,256]{1,0:T(8,128)(2,1)S(1)} %get-tuple-element.43), channel_id=1, source_target_pairs={{0,24},{4,28},{8,16},{12,20},{16,8},{20,12},{24,0},{28,4},{1,25},{... | collective-permute-start | bytes 1769480 | tf_op jit(solution)/shard_map/ppermute | solution.py:328
  6.1 7.4 %collective-permute-start = (bf16[40,1152]{1,0:T(8,128)(2,1)S(1)}, bf16[40,1152]{1,0:T(8,128)(2,1)S(1)}, u32[]{:S(2)}, u32[]{:S(2)}) collective-permute-start(bf16[40,1152]{1,0:T(8,128)(2,1)S(1)} %get-tuple-element.34), channel_id=1, source_target_pairs={{0,3},{1,2},{2,1},{3,0},{4,7},{5,6},{6,5},{7,4},{8,11},{9,10},{10,... | collective-permute-start | bytes 276488 | tf_op jit(solution)/shard_map/ppermute | solution.py:328
  9.7 8.1 %collective-permute-start.1 = (bf16[40,1152]{1,0:T(8,128)(2,1)S(1)}, bf16[40,1152]{1,0:T(8,128)(2,1)S(1)}, u32[]{:S(2)}, u32[]{:S(2)}) collective-permute-start(bf16[40,1152]{1,0:T(8,128)(2,1)S(1)} %get-tuple-element.35), channel_id=1, source_target_pairs={{0,2},{1,3},{2,0},{3,1},{4,6},{5,7},{6,4},{7,5},{8,10},{9,11},{10,... | collective-permute-start | bytes 276488 | tf_op jit(solution)/shard_map/ppermute | solution.py:328
  9.7 8.1 %collective-permute-start.2 = (bf16[40,1152]{1,0:T(8,128)(2,1)S(1)}, bf16[40,1152]{1,0:T(8,128)(2,1)S(1)}, u32[]{:S(2)}, u32[]{:S(2)}) collective-permute-start(bf16[40,1152]{1,0:T(8,128)(2,1)S(1)} %get-tuple-element.36), channel_id=1, source_target_pairs={{0,1},{1,0},{2,3},{3,2},{4,5},{5,4},{6,7},{7,6},{8,9},{9,8},{10,11... | collective-permute-start | bytes 276488 | tf_op jit(solution)/shard_map/ppermute | solution.py:328
  18.3 11.2 %collective-permute-start.7 = (bf16[80,2176]{1,0:T(8,128)(2,1)S(1)}, bf16[80,2176]{1,0:T(8,128)(2,1)S(1)}, u32[]{:S(2)}, u32[]{:S(2)}) collective-permute-start(bf16[80,2176]{1,0:T(8,128)(2,1)S(1)} %get-tuple-element.54.pq_ref), channel_id=1, source_target_pairs={{0,8},{4,12},{8,0},{12,4},{16,24},{20,28},{24,16},{28,20},{1,9},{5... | collective-permute-start | bytes 1044488 | tf_op jit(solution)/shard_map/ppermute | solution.py:328
  18.9 90.1 %collective-permute-start.8 = (bf16[80,2176]{1,0:T(8,128)(2,1)S(1)}, bf16[80,2176]{1,0:T(8,128)(2,1)S(1)}, u32[]{:S(2)}, u32[]{:S(2)}) collective-permute-start(bf16[80,2176]{1,0:T(8,128)(2,1)S(1)} %get-tuple-element.54.pq_ref), channel_id=1, source_target_pairs={{0,16},{4,20},{8,24},{12,28},{16,0},{20,4},{24,8},{28,12},{1,17},{... | collective-permute-start | bytes 1044488 | tf_op jit(solution)/shard_map/ppermute | solution.py:328
  20.1 3.7 %collective-permute-start.5 = (bf16[576,256]{1,0:T(8,128)(2,1)S(1)}, bf16[576,256]{1,0:T(8,128)(2,1)S(1)}, u32[]{:S(2)}, u32[]{:S(2)}) collective-permute-start(bf16[576,256]{1,0:T(8,128)(2,1)S(1)} %get-tuple-element.64), channel_id=1, source_target_pairs={{0,4},{4,0},{8,12},{12,8},{16,20},{20,16},{24,28},{28,24},{1,5},{5... | collective-permute-start | bytes 884744 | tf_op jit(solution)/shard_map/ppermute | solution.py:328
  20.2 3.9 %copy-start = (s32[4]{0:T(128)S(1)}, s32[4]{0:T(128)}, u32[]{:S(2)}) copy-start(s32[4]{0:T(128)} %len_ref.11) | copy-start | bytes 52
  20.2 3.6 %collective-permute-start.6 = (bf16[576,256]{1,0:T(8,128)(2,1)S(1)}, bf16[576,256]{1,0:T(8,128)(2,1)S(1)}, u32[]{:S(2)}, u32[]{:S(2)}) collective-permute-start(bf16[576,256]{1,0:T(8,128)(2,1)S(1)} %get-tuple-element.63), channel_id=1, source_target_pairs={{0,4},{4,0},{8,12},{12,8},{16,20},{20,16},{24,28},{28,24},{1,5},{5... | collective-permute-start | bytes 884744 | tf_op jit(solution)/shard_map/ppermute | solution.py:328
  20.7 168.0 %collective-permute-start.9 = (bf16[80,2176]{1,0:T(8,128)(2,1)S(1)}, bf16[80,2176]{1,0:T(8,128)(2,1)S(1)}, u32[]{:S(2)}, u32[]{:S(2)}) collective-permute-start(bf16[80,2176]{1,0:T(8,128)(2,1)S(1)} %get-tuple-element.54.pq_ref), channel_id=1, source_target_pairs={{0,24},{4,28},{8,16},{12,20},{16,8},{20,12},{24,0},{28,4},{1,25},{... | collective-permute-start | bytes 1044488 | tf_op jit(solution)/shard_map/ppermute | solution.py:328
  109.0 133.3 %collective-permute-start.10 = (bf16[136,1280]{1,0:T(8,128)(2,1)S(1)}, bf16[136,1280]{1,0:T(8,128)(2,1)S(1)}, u32[]{:S(2)}, u32[]{:S(2)}) collective-permute-start(bf16[136,1280]{1,0:T(8,128)(2,1)S(1)} %flash.7), channel_id=1, source_target_pairs={{0,8},{4,12},{8,0},{12,4},{16,24},{20,28},{24,16},{28,20},{1,9},{5... | collective-permute-start | bytes 1044488 | tf_op jit(solution)/shard_map/ppermute | solution.py:328
  188.6 53.7 %collective-permute-start.11 = (bf16[136,1280]{1,0:T(8,128)(2,1)S(1)}, bf16[136,1280]{1,0:T(8,128)(2,1)S(1)}, u32[]{:S(2)}, u32[]{:S(2)}) collective-permute-start(bf16[136,1280]{1,0:T(8,128)(2,1)S(1)} %flash.8), channel_id=1, source_target_pairs={{0,16},{4,20},{8,24},{12,28},{16,0},{20,4},{24,8},{28,12},{1,17},{... | collective-permute-start | bytes 1044488 | tf_op jit(solution)/shard_map/ppermute | solution.py:328
  238.0 8.3 %collective-permute-start.12 = (bf16[136,768]{1,0:T(8,128)(2,1)S(1)}, bf16[136,768]{1,0:T(8,128)(2,1)S(1)}, u32[]{:S(2)}, u32[]{:S(2)}) collective-permute-start(bf16[136,768]{1,0:T(8,128)(2,1)S(1)} %flash.9), channel_id=1, source_target_pairs={{0,24},{4,28},{8,16},{12,20},{16,8},{20,12},{24,0},{28,4},{1,25},{... | collective-permute-start | bytes 626696 | tf_op jit(solution)/shard_map/ppermute | solution.py:328
  239.3 7.0 %collective-permute-start.13 = (bf16[136,512]{1,0:T(8,128)(2,1)S(1)}, bf16[136,512]{1,0:T(8,128)(2,1)S(1)}, u32[]{:S(2)}, u32[]{:S(2)}) collective-permute-start(bf16[136,512]{1,0:T(8,128)(2,1)S(1)} %flash.10), channel_id=1, source_target_pairs={{0,24},{4,28},{8,16},{12,20},{16,8},{20,12},{24,0},{28,4},{1,25},{... | collective-permute-start | bytes 417800 | tf_op jit(solution)/shard_map/ppermute | solution.py:328
  246.9 107.6 %collective-permute-start.14 = (bf16[40,1024]{1,0:T(8,128)(2,1)S(1)}, bf16[40,1024]{1,0:T(8,128)(2,1)S(1)}, u32[]{:S(2)}, u32[]{:S(2)}) collective-permute-start(bf16[40,1024]{1,0:T(8,128)(2,1)S(1)} %get-tuple-element.58), channel_id=1, source_target_pairs={{0,3},{1,2},{2,1},{3,0},{4,7},{5,6},{6,5},{7,4},{8,11},{9,10},{10,... | collective-permute-start | bytes 245768 | tf_op jit(solution)/shard_map/ppermute | solution.py:328
  352.1 5.3 %collective-permute-start.15 = (bf16[40,1024]{1,0:T(8,128)(2,1)S(1)}, bf16[40,1024]{1,0:T(8,128)(2,1)S(1)}, u32[]{:S(2)}, u32[]{:S(2)}) collective-permute-start(bf16[40,1024]{1,0:T(8,128)(2,1)S(1)} %get-tuple-element.59), channel_id=1, source_target_pairs={{0,2},{1,3},{2,0},{3,1},{4,6},{5,7},{6,4},{7,5},{8,10},{9,11},{10,... | collective-permute-start | bytes 245768 | tf_op jit(solution)/shard_map/ppermute | solution.py:328
  352.1 5.3 %collective-permute-start.16 = (bf16[40,1024]{1,0:T(8,128)(2,1)S(1)}, bf16[40,1024]{1,0:T(8,128)(2,1)S(1)}, u32[]{:S(2)}, u32[]{:S(2)}) collective-permute-start(bf16[40,1024]{1,0:T(8,128)(2,1)S(1)} %get-tuple-element.60), channel_id=1, source_target_pairs={{0,1},{1,0},{2,3},{3,2},{4,5},{5,4},{6,7},{7,6},{8,9},{9,8},{10,11... | collective-permute-start | bytes 245768 | tf_op jit(solution)/shard_map/ppermute | solution.py:328

commit v4 on v3

--- a/solution.py
+++ b/solution.py
@@ -63,10 +63,8 @@
 
 def route_kernel(capacity, me_ref, req_hbm, pos_hbm, q_hbm, shard_hbm, *outs):
     outs, (req_ref, pos_ref, q_ref, sem) = outs[:-4], outs[-4:]
-    sends, back_ref, halves = outs[:-3], outs[-3], outs[-2:]
-    half = halves[0].shape[0]
-    moves = [(req_hbm, req_ref), (pos_hbm, pos_ref), (q_hbm, q_ref)]
-    moves += [(shard_hbm.at[pl.ds(i * half, half)], halves[i]) for i in range(2)]
+    sends, back_ref, shard_ref = outs[:-2], outs[-2], outs[-1]
+    moves = [(req_hbm, req_ref), (pos_hbm, pos_ref), (q_hbm, q_ref), (shard_hbm, shard_ref)]
     fetches = [pltpu.make_async_copy(src, dst, sem.at[i]) for i, (src, dst) in enumerate(moves)]
     for fetch in fetches:
         fetch.start()
@@ -152,40 +150,42 @@
     vt_ref[HD:, at] = (iota((vt_ref.shape[0] - HD, count), 0) == 0).astype(jnp.bfloat16)
 
 
-def keys_kernel(first, pieces, *refs):
+def keys_kernel(first, parts, own_ref, *refs):
     k_ref, vt_ref = refs[-2:]
-    at = 0
-    for number, count in enumerate(pieces, first):
-        store_keys(k_ref, vt_ref, number, jnp.concatenate([ref[...] for ref in refs[at : at + count]], axis=0))
-        at += count
-
-
-def flash_kernel(
-    first, chips, piece, me_ref, len_ref, pq_ref, k_ref, vt_ref, out_ref, q_ref, acc_ref, row_ref, s_ref, top_ref, job_ref, info_ref
-):
+    store_keys(k_ref, vt_ref, first, own_ref[...])
+    store_keys(k_ref, vt_ref, first + 1, jnp.concatenate([ref[...] for ref in refs[:parts]], axis=0))
+
+
+def flash_kernel(far, chips, piece, me_ref, len_ref, pq_ref, k_ref, vt_ref, *refs):
+    if far:
+        before_ref, out_ref, q_ref, acc_ref, row_ref, s_ref, top_ref, job_ref, info_ref = refs
+        acc_ref[...] = before_ref[...]
+    else:
+        acc_ref, q_ref, row_ref, s_ref, job_ref, info_ref = refs
+        acc_ref[...] = jnp.zeros_like(acc_ref)
     width = TILE * H
-    all_width = out_ref.shape[1]
-    tiles = all_width // width
+    tiles = pq_ref.shape[0] // TILE
+    all_width = tiles * width
     pieces = 4
     length = len_ref[me_ref[1]]
     chip, core = me_ref[0] // 2, lax.rem(me_ref[0], 2)
-    home_at = chip * (4 * piece)
-    away_at = (chips - 1 - chip) * (4 * piece) + piece
-    rising = home_at < away_at
-    for pair, kept in enumerate((rising, jnp.logical_not(rising))):
-        for k in range(2):
-            info_ref[2 * pair + k] = jnp.where(kept, home_at, away_at) + 2 * piece * k
-            info_ref[pieces + 2 * pair + k] = jnp.where(kept, 0, 2) + jnp.where(core == k, 0, 1)
-    meta = pq_ref[first * TILE : (first + tiles) * TILE, WIDE:].astype(jnp.float32)
+    for k in range(pieces):
+        number = jnp.where(core == k // 2, 0, 2) + k % 2
+        for base, at in ((0, chip), (2 * pieces, lax.rem(chip + chips // 2, chips))):
+            info_ref[base + k] = at * (4 * piece) + piece * k
+            info_ref[base + pieces + k] = number + base // 2
+    base = 2 * pieces if far else 0
+    meta = pq_ref[:, WIDE:].astype(jnp.float32)
     pos = meta[:, 0:1] * 256.0 + meta[:, 1:2] - 1.0
     last = jnp.minimum(pos, (length - 1).astype(jnp.float32))
     tops, lows = [], []
     for j in range(tiles):
+        tops.append(last[j * TILE, 0].astype(jnp.int32))
+        lows.append(last[(j + 1) * TILE - 1, 0].astype(jnp.int32))
+    for j in range(tiles):
         here = last[j * TILE : (j + 1) * TILE]
-        tops.append(jnp.max(here).astype(jnp.int32))
-        lows.append(jnp.min(here).astype(jnp.int32))
         row_ref[0:1, j * width : (j + 1) * width] = jnp.concatenate([row_of(here)] * H, axis=1)
-        rows = slice((first + j) * TILE, (first + j + 1) * TILE)
+        rows = slice(j * TILE, (j + 1) * TILE)
         for h in range(H):
             x = pq_ref[rows, h * HD : (h + 1) * HD].astype(jnp.float32) * EXP_SCALE
             high = x.astype(jnp.bfloat16)
@@ -195,26 +195,25 @@
     count, whole = jnp.int32(0), []
     for j in range(tiles):
         for i in range(pieces):
-            whole.append(info_ref[i] + (piece - 1) <= lows[j])
+            whole.append(info_ref[base + i] + (piece - 1) <= lows[j])
             job_ref[count] = j * pieces + i
             count += whole[-1].astype(jnp.int32)
     whole_turns = count // 2
     for j in range(tiles):
         for i in range(pieces):
             job_ref[count] = j * pieces + i
-            count += ((info_ref[i] <= tops[j]) & jnp.logical_not(whole[j * pieces + i])).astype(jnp.int32)
+            count += ((info_ref[base + i] <= tops[j]) & jnp.logical_not(whole[j * pieces + i])).astype(jnp.int32)
     for k in range(3):
         job_ref[count + k] = tiles * pieces
     row_ref[0:1, all_width:] = jnp.full((1, width), -1.0, jnp.float32)
     q_ref[all_width:, :] = jnp.zeros((width, 2 * HD), jnp.bfloat16)
-    acc_ref[...] = jnp.zeros_like(acc_ref)
 
     def place(job):
         tile = job // pieces
-        return pl.ds(pl.multiple_of(tile * width, width), width), job - tile * pieces
+        return pl.ds(pl.multiple_of(tile * width, width), width), job - tile * pieces + base
 
     def keys(c, a, n):
-        return pl.ds(pl.multiple_of(info_ref[pieces + c] * piece + a, 128), n)
+        return pl.ds(pl.multiple_of(info_ref[c + pieces] * piece + a, 128), n)
 
     def scores(cols, c, a, n):
         return dot(k_ref[keys(c, a, n), :], q_ref[cols, :], NT)
@@ -253,9 +252,11 @@
 
     pl.loop(0, whole_turns)(lambda b: turn(b, False))
     pl.loop(whole_turns, (count + 1) // 2)(lambda b: turn(b, True))
+    if not far:
+        return
     top_ref[0:1, :] = jnp.zeros((1, all_width), jnp.float32)
     total = acc_ref[HD : HD + 1, :all_width]
-    dead = row_ref[0:1, :all_width] < info_ref[0].astype(jnp.float32)
+    dead = row_ref[0:1, :all_width] < jnp.minimum(info_ref[0], info_ref[base]).astype(jnp.float32)
     fine = dead | ((total > 2.0**-60) & (total < 2.0**100))
 
     @pl.when(jnp.logical_not(jnp.min(fine.astype(jnp.float32)) > 0.5))
@@ -265,8 +266,9 @@
 
         def careful(i, carry):
             chunks = piece // 128
-            cols = pl.ds(pl.multiple_of(i // (pieces * chunks) * width, width), width)
-            c, a = i % (pieces * chunks) // chunks, i % chunks * 128
+            cols = pl.ds(pl.multiple_of(i // (2 * pieces * chunks) * width, width), width)
+            c, a = i // chunks % (2 * pieces), i % chunks * 128
+            c += jnp.where(c < pieces, 0, pieces)
             s = masked(scores(cols, c, a, 128), cols, c, a)
             before = top_ref[0:1, cols]
             after = jnp.maximum(before, jnp.max(s, axis=0, keepdims=True))
@@ -275,7 +277,7 @@
             top_ref[0:1, cols] = after
             return carry
 
-        lax.fori_loop(0, tiles * pieces * (piece // 128), careful, 0)
+        lax.fori_loop(0, tiles * 2 * pieces * (piece // 128), careful, 0)
 
     total = acc_ref[HD : HD + 1, :all_width]
     some = total > 0.0
@@ -344,25 +346,25 @@
     me = jnp.stack([here, mine]).astype(jnp.int32)
     bf = lambda *shape: jax.ShapeDtypeStruct(shape, jnp.bfloat16)
 
-    *sends, back_tok, kept, away = call(
+    *sends, back_tok, shard = call(
         functools.partial(route_kernel, capacity),
-        [bf(block, width + META)] * groups + [bf(fold, tok_rows, groups * block)] + [bf(half, 2 * HD)] * 2,
+        [bf(block, width + META)] * groups + [bf(fold, tok_rows, groups * block)] + [bf(shard_len, 2 * HD)],
         [SMEM] + [pl.BlockSpec(memory_space=pltpu.HBM)] * 4,
         "route",
         scratch=[
             pltpu.VMEM((1, tok_rows), jnp.int32),
             pltpu.VMEM((1, tok_rows), jnp.int32),
             pltpu.VMEM((tok_rows, WIDE), jnp.bfloat16),
-            pltpu.SemaphoreType.DMA((5,)),
+            pltpu.SemaphoreType.DMA((4,)),
         ],
     )(me, *[in_hbm(x) for x in (req_of.reshape(1, tok_rows), q_pos.reshape(1, tok_rows), queries, cache[0])])
     blocks = {d: swapped(sends[d], "req", d) for d in reversed(range(1, groups))}
     blocks[0] = sends[0]
-    away = swapped(away, "ctx", cycle - 2)
-    kept_sib = swapped(kept, "ctx", 1)
-    all_keys = [bf(4 * half, 2 * HD), bf(HD + 16, 4 * half)]
-    kept_keys = call(functools.partial(keys_kernel, 0, (1, 1)), all_keys, [VMEM] * 2, "kept_keys")(kept, kept_sib)
-    blocks[0], *kept_keys = lax.optimization_barrier((blocks[0], *kept_keys))
+    far_shard = swapped(shard, "ctx", cycle // 2)
+    sibling = swapped(shard, "ctx", 1)
+    all_keys = [bf(4 * shard_len, 2 * HD), bf(HD + 16, 4 * shard_len)]
+    keys = call(functools.partial(keys_kernel, 0, 1), all_keys, [VMEM] * 2, "home_keys")(shard, sibling)
+    blocks[0], *keys = lax.optimization_barrier((blocks[0], *keys))
 
     sorted_q, back_slot = call(
         functools.partial(sort_kernel, capacity),
@@ -370,48 +372,47 @@
         [VMEM] * groups,
         "sort",
     )(*[blocks[d] for d in reversed(range(groups))])
-    visiting = {d: swapped(sorted_q, "ctx", 2 * d) for d in range(1, chips)}
-    sorted_q, away = lax.optimization_barrier((sorted_q, away))
-    away_sib = [swapped(away[i * half // 2 : (i + 1) * half // 2], "ctx", 1) for i in range(2)]
-
-    k_all, vt_all = call(
-        functools.partial(keys_kernel, 2, (1, 2)), all_keys, [VMEM] * 5, "away_keys", aliases={3: 0, 4: 1}
-    )(away, *away_sib, *kept_keys)
-
-    def flash(q, first=0, tiles=slots // TILE):
-        extra = (tiles + 1) * TILE * H
+    visiting = {d: swapped(sorted_q, "ctx", 2 * d) for d in range(1, chips // 2)}
+
+    def flash(q, keys, before=None):
+        far = before is not None
+        extra = (slots + TILE) * H
+        sums = jax.ShapeDtypeStruct((HD + 16, extra), jnp.float32)
+        scratch = [
+            pltpu.VMEM((extra, 2 * HD), jnp.bfloat16),
+            pltpu.VMEM(sums.shape, sums.dtype),
+            pltpu.VMEM((8, extra), jnp.float32),
+            pltpu.VMEM((2, SUB, TILE * H), jnp.float32),
+            pltpu.VMEM((8, slots * H), jnp.float32),
+            pltpu.SMEM((4 * slots // TILE + 4,), jnp.int32),
+            pltpu.SMEM((16,), jnp.int32),
+        ]
         return call(
-            functools.partial(flash_kernel, first, chips, half),
-            bf(OUT_ROWS, tiles * TILE * H),
-            [SMEM, SMEM] + [VMEM] * 3,
-            "flash",
-            scratch=[
-                pltpu.VMEM((extra, 2 * HD), jnp.bfloat16),
-                pltpu.VMEM((HD + 16, extra), jnp.float32),
-                pltpu.VMEM((8, extra), jnp.float32),
-                pltpu.VMEM((2, SUB, TILE * H), jnp.float32),
-                pltpu.VMEM((8, tiles * TILE * H), jnp.float32),
-                pltpu.SMEM((4 * tiles + 4,), jnp.int32),
-                pltpu.SMEM((8,), jnp.int32),
-            ],
-        )(me, cache_len, q, k_all, vt_all)
-
-    tiles = slots // TILE
-    last = max(visiting, key=lambda d: (d & (d - 1) != 0, d))
-    turn = flash(sorted_q, 0, 2)
-    own, home = [turn], {}
-    for d in sorted(visiting, key=lambda d: (d == last, d & (d - 1) != 0, d)):
-        home[d] = []
-        for at, count in ((0, 3), (3, tiles - 3)) if d == last else ((0, tiles),):
-            turn, q = lax.optimization_barrier((turn, visiting[d]))
-            turn = flash(q, at, count)
-            home[d].append(swapped(turn, "ctx", 2 * d))
-    before = [home[d][0] for d in home if d != last]
-    turn, q, *before = lax.optimization_barrier((turn, sorted_q, *before))
-    own.append(flash(q, 2, tiles - 2))
-    home = [own, home[last], *[[part] for part in before]]
-    cuts = tuple(len(part) for part in home)
-    home = [ref for part in home for ref in part]
+            functools.partial(flash_kernel, far, chips, half),
+            bf(OUT_ROWS, slots * H) if far else sums,
+            [SMEM, SMEM] + [VMEM] * (4 if far else 3),
+            "flash_far" if far else "flash_home",
+            scratch=scratch if far else [scratch[i] for i in (0, 2, 3, 5, 6)],
+        )(me, cache_len, q, *keys, *([before] if far else []))
+
+    turn = flash(sorted_q, keys)
+    sums = {0: turn}
+    for d in visiting:
+        turn, visiting[d] = lax.optimization_barrier((turn, visiting[d]))
+        turn = sums[d] = flash(visiting[d], keys)
+    turn, far_shard, *keys = lax.optimization_barrier((turn, far_shard, *keys))
+    far_sibling = [swapped(far_shard[i * half : (i + 1) * half], "ctx", 1) for i in range(2)]
+    keys = call(
+        functools.partial(keys_kernel, 2, 2), all_keys, [VMEM] * 5, "far_keys", aliases={3: 0, 4: 1}
+    )(far_shard, *far_sibling, *keys)
+    home = []
+    for d in visiting:
+        turn, q = lax.optimization_barrier((turn, visiting[d]))
+        turn = flash(q, keys, sums[d])
+        home.append(swapped(turn, "ctx", 2 * d))
+    turn, q = lax.optimization_barrier((turn, sorted_q))
+    home.append(flash(q, keys, sums[0]))
+    cuts = (1,) * len(home)
     outs = call(
         functools.partial(merge_kernel, cuts),
         [bf(block, width)] * groups,

time: 360 us -> 362 us (level); the launches traced: 358 us -> 356 us
  starting transfers between devices: 122 us -> 17.9 us
  Pallas kernels: 220 us -> 323 us
    ppermute x17 -> x12, starting transfers between devices: 122 us -> 17.9 us  [swapped(): return lax.ppermute(block, axis, [(i, i ^ distance) for i in devices])]
    pallas_call x8 -> x6, Pallas kernels: 216 us -> 319 us  [the longest x4 318 us: flash(): call(functools.partial(flash_kernel, far, chips, half), bf(OUT_ROWS, slot...]
    ppermute x17 -> x12, waiting for transfers between devices: 15.8 us -> 14.8 us  [swapped(): return lax.ppermute(block, axis, [(i, i ^ distance) for i in devices])]
  transfers between devices with their start and end apart: 17 -> 12, of which waited for: 7 -> 6; matrix products, arithmetic and copies ran while one was open for 0% -> 0% of each run, Pallas kernels for 60% -> 47%
where the time goes in v4:
time: 362 us; the launch traced here: 356 us
  Pallas kernels  323 us (89%)
  starting transfers between devices  17.9 us (5%)
  waiting for transfers between devices  14.8 us (4%)
    pallas_call x4, Pallas kernels, flash(): call(functools.partial(flash_kernel, far, chips, half), bf(OUT_ROWS, slot...  318 us
    ppermute x12, starting transfers between devices, swapped(): return lax.ppermute(block, axis, [(i, i ^ distance) for i in devices])  17.9 us
    ppermute x12, waiting for transfers between devices, swapped(): return lax.ppermute(block, axis, [(i, i ^ distance) for i in devices])  14.8 us
  transfers between devices with their start and end apart: 12, of which 6 were waited for; matrix products, arithmetic and copies ran while one was open for 0% of the time, Pallas kernels for 47%

profile of v4, /device:TPU:0, one launch (start us, length us, event | category | flops | bytes accessed | tf_op | source)
XLA Modules:
  0.0 355.8 jit_solution(15461118096491449028)
XLA Ops:
  0.0 0.1 pad_add_fusion.me_ref
  0.1 2.0 route.1
  2.1 0.5 collective-permute-start.3
  2.6 2.6 collective-permute-start.5
  5.2 3.6 %collective-permute-start = (bf16[40,1152]{1,0:T(8,128)(2,1)S(1)}, bf16[40,1152]{1,0:T(8,128)(2,1)S(1)}, u32[]{:S(2)}, u32[]{:S(2)}) collective-permute-start(bf16[40,1152]{1,0:T(8,128)(2,1)S(1)} %get-tuple-element.29), channel_id=1, source_target_pairs={{0,3},{1,2},{2,1},{3,0},{4,7},{5,6},{6,5},{7,4},{8,11},{9,10},{10,... | collective-permute-start | bytes 276488 | tf_op jit(solution)/shard_map/ppermute | solution.py:330
  8.8 0.0 collective-permute-start.1
  8.8 0.8 collective-permute-start.2
  9.6 0.0 collective-permute-done.3.refs_0_
  9.6 0.6 home_keys.1
  10.1 2.4 collective-permute-done.refs_0_
  12.5 4.3 %collective-permute-done.1.refs_1_ = bf16[40,1152]{1,0:T(8,128)(2,1)S(1)} collective-permute-done((bf16[40,1152]{1,0:T(8,128)(2,1)S(1)}, bf16[40,1152]{1,0:T(8,128)(2,1)S(1)}, u32[]{:S(2)}, u32[]{:S(2)}) %collective-permute-start.1) | collective-permute-done | bytes 92192 | tf_op jit(solution)/shard_map/ppermute | solution.py:330
  16.9 0.0 collective-permute-done.2.refs_2_
  16.9 0.5 sort.1
  17.4 1.6 collective-permute-start.4
  19.0 8.4 %flash_home.2.refs_0_ = f32[144,1536]{1,0:T(8,128)S(1)} custom-call(s32[2]{0:T(128)S(1)} %pad_add_fusion.me_ref, s32[4]{0:T(128)S(1)} %copy-done, bf16[80,2176]{1,0:T(8,128)(2,1)S(1)} %get-tuple-element.46.pq_ref, bf16[9216,256]{1,0:T(8,128)(2,1)S(1)} %get-tuple-element.42.k_ref.refs_2_, bf16[144,9216]{1,0:T(8,128)(2,1)S(1)} %get-tuple-element.43.vt_ref.refs_3_), custom_call_target="tpu_custom_call" | custom-call | flops 1 | bytes 1 | tf_op jit(solution)/shard_map/flash_home/pallas_call | solution.py:390
  27.3 9.1 %flash_home.3.refs_0_ = f32[144,1536]{1,0:T(8,128)S(1)} custom-call(s32[2]{0:T(128)S(1)} %pad_add_fusion.me_ref, s32[4]{0:T(128)S(1)} %copy-done, bf16[80,2176]{1,0:T(8,128)(2,1)S(1)} %collective-permute-done.4.pq_ref, bf16[9216,256]{1,0:T(8,128)(2,1)S(1)} %get-tuple-element.42.k_ref.refs_2_, bf16[144,9216]{1,0:T(8,128)(2,1)S(1)} %get-tuple-element.43.vt_ref.refs_3_), custom_call_target="tpu_custom_call" | custom-call | flops 1 | bytes 1 | tf_op jit(solution)/shard_map/flash_home/pallas_call | solution.py:390
  36.5 0.1 fusion
  36.5 0.1 collective-permute-start.7
  36.6 0.5 collective-permute-start.6
  37.1 1.5 collective-permute-done.7.refs_1_
  38.6 0.8 collective-permute-done.6.refs_0_
  39.5 0.5 far_keys.1
  40.0 150.2 %flash_far.2 = bf16[136,1280]{1,0:T(8,128)(2,1)S(1)} custom-call(s32[2]{0:T(128)S(1)} %pad_add_fusion.me_ref, s32[4]{0:T(128)S(1)} %copy-done, bf16[80,2176]{1,0:T(8,128)(2,1)S(1)} %collective-permute-done.4.pq_ref, bf16[9216,256]{1,0:T(8,128)(2,1)S(1)} %get-tuple-element.44.k_ref, bf16[144,9216]{1,0:T(8,128)(2,1)S(1)} %get-tuple-element.45.vt_ref, ...), custom_call_target="tpu_custom_call" | custom-call | flops 1 | bytes 1 | tf_op jit(solution)/shard_map/flash_far/pallas_call | solution.py:390
  190.2 0.1 collective-permute-start.8
  190.3 150.2 %flash_far.3.refs_1_ = bf16[136,1280]{1,0:T(8,128)(2,1)S(1)} custom-call(s32[2]{0:T(128)S(1)} %pad_add_fusion.me_ref, s32[4]{0:T(128)S(1)} %copy-done, bf16[80,2176]{1,0:T(8,128)(2,1)S(1)} %get-tuple-element.46.pq_ref, bf16[9216,256]{1,0:T(8,128)(2,1)S(1)} %get-tuple-element.44.k_ref, bf16[144,9216]{1,0:T(8,128)(2,1)S(1)} %get-tuple-element.45.vt_ref, ...), custom_call_target="tpu_custom_call" | custom-call | flops 1 | bytes 1 | tf_op jit(solution)/shard_map/flash_far/pallas_call | solution.py:390
  340.4 0.5 merge.1
  340.9 7.5 %collective-permute-start.9 = (bf16[40,1024]{1,0:T(8,128)(2,1)S(1)}, bf16[40,1024]{1,0:T(8,128)(2,1)S(1)}, u32[]{:S(2)}, u32[]{:S(2)}) collective-permute-start(bf16[40,1024]{1,0:T(8,128)(2,1)S(1)} %get-tuple-element.48), channel_id=1, source_target_pairs={{0,3},{1,2},{2,1},{3,0},{4,7},{5,6},{6,5},{7,4},{8,11},{9,10},{10,... | collective-permute-start | bytes 245768 | tf_op jit(solution)/shard_map/ppermute | solution.py:330
  348.5 0.6 collective-permute-start.11
  349.1 2.6 collective-permute-done.9.refs_0_
  351.7 3.1 collective-permute-done.10.refs_1_
  354.8 0.0 collective-permute-done.11.refs_2_
  354.8 1.0 unroute.1
  (6 shorter events, 0.0 us)
Async XLA Ops:
  2.1 7.5 %collective-permute-start.3 = (bf16[2304,256]{1,0:T(8,128)(2,1)S(1)}, bf16[2304,256]{1,0:T(8,128)(2,1)S(1)}, u32[]{:S(2)}, u32[]{:S(2)}) collective-permute-start(bf16[2304,256]{1,0:T(8,128)(2,1)S(1)} %get-tuple-element.33.own_ref), channel_id=1, source_target_pairs={{0,4},{4,0},{8,12},{12,8},{16,20},{20,16},{24,28},{28,24},{1,5},{5... | collective-permute-start | bytes 3538952 | tf_op jit(solution)/shard_map/ppermute | solution.py:330
  2.6 33.9 %collective-permute-start.5 = (bf16[2304,256]{1,0:T(8,128)(2,1)S(1)}, bf16[2304,256]{1,0:T(8,128)(2,1)S(1)}, u32[]{:S(2)}, u32[]{:S(2)}) collective-permute-start(bf16[2304,256]{1,0:T(8,128)(2,1)S(1)} %get-tuple-element.33.own_ref), channel_id=1, source_target_pairs={{0,16},{4,20},{8,24},{12,28},{16,0},{20,4},{24,8},{28,12},{1,17},{... | collective-permute-start | bytes 3538952 | tf_op jit(solution)/shard_map/ppermute | solution.py:330
  5.2 7.4 %collective-permute-start = (bf16[40,1152]{1,0:T(8,128)(2,1)S(1)}, bf16[40,1152]{1,0:T(8,128)(2,1)S(1)}, u32[]{:S(2)}, u32[]{:S(2)}) collective-permute-start(bf16[40,1152]{1,0:T(8,128)(2,1)S(1)} %get-tuple-element.29), channel_id=1, source_target_pairs={{0,3},{1,2},{2,1},{3,0},{4,7},{5,6},{6,5},{7,4},{8,11},{9,10},{10,... | collective-permute-start | bytes 276488 | tf_op jit(solution)/shard_map/ppermute | solution.py:330
  8.8 8.1 %collective-permute-start.1 = (bf16[40,1152]{1,0:T(8,128)(2,1)S(1)}, bf16[40,1152]{1,0:T(8,128)(2,1)S(1)}, u32[]{:S(2)}, u32[]{:S(2)}) collective-permute-start(bf16[40,1152]{1,0:T(8,128)(2,1)S(1)} %get-tuple-element.30), channel_id=1, source_target_pairs={{0,2},{1,3},{2,0},{3,1},{4,6},{5,7},{6,4},{7,5},{8,10},{9,11},{10,... | collective-permute-start | bytes 276488 | tf_op jit(solution)/shard_map/ppermute | solution.py:330
  8.8 10.2 %copy-start = (s32[4]{0:T(128)S(1)}, s32[4]{0:T(128)}, u32[]{:S(2)}) copy-start(s32[4]{0:T(128)} %len_ref.7) | copy-start | bytes 52
  8.8 8.1 %collective-permute-start.2 = (bf16[40,1152]{1,0:T(8,128)(2,1)S(1)}, bf16[40,1152]{1,0:T(8,128)(2,1)S(1)}, u32[]{:S(2)}, u32[]{:S(2)}) collective-permute-start(bf16[40,1152]{1,0:T(8,128)(2,1)S(1)} %get-tuple-element.31), channel_id=1, source_target_pairs={{0,1},{1,0},{2,3},{3,2},{4,5},{5,4},{6,7},{7,6},{8,9},{9,8},{10,11... | collective-permute-start | bytes 276488 | tf_op jit(solution)/shard_map/ppermute | solution.py:330
  17.4 9.9 %collective-permute-start.4 = (bf16[80,2176]{1,0:T(8,128)(2,1)S(1)}, bf16[80,2176]{1,0:T(8,128)(2,1)S(1)}, u32[]{:S(2)}, u32[]{:S(2)}) collective-permute-start(bf16[80,2176]{1,0:T(8,128)(2,1)S(1)} %get-tuple-element.46.pq_ref), channel_id=1, source_target_pairs={{0,8},{4,12},{8,0},{12,4},{16,24},{20,28},{24,16},{28,20},{1,9},{5... | collective-permute-start | bytes 1044488 | tf_op jit(solution)/shard_map/ppermute | solution.py:330
  36.5 2.1 collective-permute-start.7
  36.6 2.8 collective-permute-start.6
  190.2 150.3 %collective-permute-start.8 = (bf16[136,1280]{1,0:T(8,128)(2,1)S(1)}, bf16[136,1280]{1,0:T(8,128)(2,1)S(1)}, u32[]{:S(2)}, u32[]{:S(2)}) collective-permute-start(bf16[136,1280]{1,0:T(8,128)(2,1)S(1)} %flash_far.2), channel_id=1, source_target_pairs={{0,8},{4,12},{8,0},{12,4},{16,24},{20,28},{24,16},{28,20},{1,9},{5... | collective-permute-start | bytes 1044488 | tf_op jit(solution)/shard_map/ppermute | solution.py:330
  340.9 10.8 %collective-permute-start.9 = (bf16[40,1024]{1,0:T(8,128)(2,1)S(1)}, bf16[40,1024]{1,0:T(8,128)(2,1)S(1)}, u32[]{:S(2)}, u32[]{:S(2)}) collective-permute-start(bf16[40,1024]{1,0:T(8,128)(2,1)S(1)} %get-tuple-element.48), channel_id=1, source_target_pairs={{0,3},{1,2},{2,1},{3,0},{4,7},{5,6},{6,5},{7,4},{8,11},{9,10},{10,... | collective-permute-start | bytes 245768 | tf_op jit(solution)/shard_map/ppermute | solution.py:330
  348.5 6.3 %collective-permute-start.10 = (bf16[40,1024]{1,0:T(8,128)(2,1)S(1)}, bf16[40,1024]{1,0:T(8,128)(2,1)S(1)}, u32[]{:S(2)}, u32[]{:S(2)}) collective-permute-start(bf16[40,1024]{1,0:T(8,128)(2,1)S(1)} %get-tuple-element.49), channel_id=1, source_target_pairs={{0,2},{1,3},{2,0},{3,1},{4,6},{5,7},{6,4},{7,5},{8,10},{9,11},{10,... | collective-permute-start | bytes 245768 | tf_op jit(solution)/shard_map/ppermute | solution.py:330
  348.5 6.3 %collective-permute-start.11 = (bf16[40,1024]{1,0:T(8,128)(2,1)S(1)}, bf16[40,1024]{1,0:T(8,128)(2,1)S(1)}, u32[]{:S(2)}, u32[]{:S(2)}) collective-permute-start(bf16[40,1024]{1,0:T(8,128)(2,1)S(1)} %get-tuple-element.50), channel_id=1, source_target_pairs={{0,1},{1,0},{2,3},{3,2},{4,5},{5,4},{6,7},{7,6},{8,9},{9,8},{10,11... | collective-permute-start | bytes 245768 | tf_op jit(solution)/shard_map/ppermute | solution.py:330

commit v5 on v4

--- a/solution.py
+++ b/solution.py
@@ -147,7 +147,6 @@
     k_ref[at, :HD] = piece[:, :HD]
     k_ref[at, HD:] = piece[:, :HD]
     vt_ref[:HD, at] = jnp.transpose(piece[:, HD:], (1, 0))
-    vt_ref[HD:, at] = (iota((vt_ref.shape[0] - HD, count), 0) == 0).astype(jnp.bfloat16)
 
 
 def keys_kernel(first, parts, own_ref, *refs):
@@ -234,21 +233,23 @@
         now = [place(job_ref[2 * b + k]) for k in range(2)]
         later = [place(job_ref[2 * b + 2 + k]) for k in range(2)]
         s = [s_ref[k] for k in range(2)]
-        totals = [None, None]
+        totals, weight_sums = [None, None], [0.0, 0.0]
         for i, (a, n) in enumerate(subs):
             if i + 1 < len(subs):
                 next_s = [scores(cols, c, *subs[i + 1]) for cols, c in now]
             else:
                 next_s = [scores(cols, c, *subs[0]) for cols, c in later]
             for k, (cols, c) in enumerate(now):
-                weights = jnp.exp2(masked(s[k], cols, c, a) if mask else s[k]).astype(jnp.bfloat16)
-                term = dot(vt_ref[:, keys(c, a, n)], weights)
+                weights = jnp.exp2(masked(s[k], cols, c, a) if mask else s[k])
+                weight_sums[k] += jnp.sum(weights, axis=0, keepdims=True)
+                term = dot(vt_ref[:, keys(c, a, n)], weights.astype(jnp.bfloat16))
                 totals[k] = term if totals[k] is None else totals[k] + term
             s = next_s
         for k in range(2):
             s_ref[k] = s[k]
         for k, (cols, _) in enumerate(now):
-            acc_ref[:, cols] += totals[k]
+            acc_ref[:HD, cols] += totals[k]
+            acc_ref[HD : HD + 1, cols] += weight_sums[k]
 
     pl.loop(0, whole_turns)(lambda b: turn(b, False))
     pl.loop(whole_turns, (count + 1) // 2)(lambda b: turn(b, True))
@@ -272,8 +273,11 @@
             s = masked(scores(cols, c, a, 128), cols, c, a)
             before = top_ref[0:1, cols]
             after = jnp.maximum(before, jnp.max(s, axis=0, keepdims=True))
-            weights = jnp.exp2(s - after).astype(jnp.bfloat16)
-            acc_ref[:, cols] = acc_ref[:, cols] * jnp.exp2(before - after) + dot(vt_ref[:, keys(c, a, 128)], weights)
+            weights = jnp.exp2(s - after)
+            shrink = jnp.exp2(before - after)
+            term = dot(vt_ref[:, keys(c, a, 128)], weights.astype(jnp.bfloat16))
+            acc_ref[:HD, cols] = acc_ref[:HD, cols] * shrink + term
+            acc_ref[HD : HD + 1, cols] = acc_ref[HD : HD + 1, cols] * shrink + jnp.sum(weights, axis=0, keepdims=True)
             top_ref[0:1, cols] = after
             return carry
 
@@ -362,7 +366,7 @@
     blocks[0] = sends[0]
     far_shard = swapped(shard, "ctx", cycle // 2)
     sibling = swapped(shard, "ctx", 1)
-    all_keys = [bf(4 * shard_len, 2 * HD), bf(HD + 16, 4 * shard_len)]
+    all_keys = [bf(4 * shard_len, 2 * HD), bf(HD, 4 * shard_len)]
     keys = call(functools.partial(keys_kernel, 0, 1), all_keys, [VMEM] * 2, "home_keys")(shard, sibling)
     blocks[0], *keys = lax.optimization_barrier((blocks[0], *keys))
 
@@ -377,7 +381,7 @@
     def flash(q, keys, before=None):
         far = before is not None
         extra = (slots + TILE) * H
-        sums = jax.ShapeDtypeStruct((HD + 16, extra), jnp.float32)
+        sums = jax.ShapeDtypeStruct((HD + 8, extra), jnp.float32)
         scratch = [
             pltpu.VMEM((extra, 2 * HD), jnp.bfloat16),
             pltpu.VMEM(sums.shape, sums.dtype),

time: 362 us -> 364 us (level)
  starting transfers between devices: 17.9 us -> 21.8 us
    ppermute x12, starting transfers between devices: 17.9 us -> 21.8 us  [swapped(): return lax.ppermute(block, axis, [(i, i ^ distance) for i in devices])]
where the time goes in v5:
time: 364 us; the launch traced here: 360 us
  Pallas kernels  323 us (89%)
  starting transfers between devices  21.8 us (6%)
  waiting for transfers between devices  15.2 us (4%)
    pallas_call x4, Pallas kernels, flash(): call(functools.partial(flash_kernel, far, chips, half), bf(OUT_ROWS, slot...  318 us
    ppermute x12, starting transfers between devices, swapped(): return lax.ppermute(block, axis, [(i, i ^ distance) for i in devices])  21.8 us
    ppermute x12, waiting for transfers between devices, swapped(): return lax.ppermute(block, axis, [(i, i ^ distance) for i in devices])  15.2 us
  transfers between devices with their start and end apart: 12, of which 6 were waited for; matrix products, arithmetic and copies ran while one was open for 0% of the time, Pallas kernels for 47%

profile of v5, /device:TPU:0, one launch (start us, length us, event | category | flops | bytes accessed | tf_op | source)
XLA Modules:
  0.0 360.3 jit_solution(13545597537112609283)
XLA Ops:
  0.0 0.1 pad_add_fusion.me_ref
  0.1 2.0 route.1
  2.1 0.5 collective-permute-start.3
  2.6 2.6 collective-permute-start.5
  5.2 3.6 collective-permute-start
  8.8 0.8 collective-permute-start.2
  9.6 0.5 home_keys.1
  10.1 2.4 collective-permute-done.refs_0_
  12.5 4.3 %collective-permute-done.1.refs_1_ = bf16[40,1152]{1,0:T(8,128)(2,1)S(1)} collective-permute-done((bf16[40,1152]{1,0:T(8,128)(2,1)S(1)}, bf16[40,1152]{1,0:T(8,128)(2,1)S(1)}, u32[]{:S(2)}, u32[]{:S(2)}) %collective-permute-start.1) | collective-permute-done | bytes 92192 | tf_op jit(solution)/shard_map/ppermute | solution.py:334
  16.9 0.0 collective-permute-done.2.refs_2_
  16.9 0.5 sort.1
  17.4 1.6 collective-permute-start.4
  19.0 7.5 %flash_home.2.refs_0_ = f32[136,1536]{1,0:T(8,128)S(1)} custom-call(s32[2]{0:T(128)S(1)} %pad_add_fusion.me_ref, s32[4]{0:T(128)S(1)} %copy-done, bf16[80,2176]{1,0:T(8,128)(2,1)S(1)} %get-tuple-element.46.pq_ref, bf16[9216,256]{1,0:T(8,128)(2,1)S(1)} %get-tuple-element.42.k_ref.refs_2_, bf16[128,9216]{1,0:T(8,128)(2,1)S(1)} %get-tuple-element.43.vt_ref.refs_3_), custom_call_target="tpu_custom_call" | custom-call | flops 1 | bytes 1 | tf_op jit(solution)/shard_map/flash_home/pallas_call | solution.py:394
  26.5 0.4 collective-permute-done.4.pq_ref
  26.9 7.5 %flash_home.3.refs_0_ = f32[136,1536]{1,0:T(8,128)S(1)} custom-call(s32[2]{0:T(128)S(1)} %pad_add_fusion.me_ref, s32[4]{0:T(128)S(1)} %copy-done, bf16[80,2176]{1,0:T(8,128)(2,1)S(1)} %collective-permute-done.4.pq_ref, bf16[9216,256]{1,0:T(8,128)(2,1)S(1)} %get-tuple-element.42.k_ref.refs_2_, bf16[128,9216]{1,0:T(8,128)(2,1)S(1)} %get-tuple-element.43.vt_ref.refs_3_), custom_call_target="tpu_custom_call" | custom-call | flops 1 | bytes 1 | tf_op jit(solution)/shard_map/flash_home/pallas_call | solution.py:394
  34.4 0.1 fusion
  34.5 0.1 collective-permute-start.7
  34.5 0.5 collective-permute-start.6
  35.0 1.5 collective-permute-done.7.refs_1_
  36.5 0.8 collective-permute-done.6.refs_0_
  37.4 0.6 far_keys.1
  37.9 151.5 %flash_far.2 = bf16[136,1280]{1,0:T(8,128)(2,1)S(1)} custom-call(s32[2]{0:T(128)S(1)} %pad_add_fusion.me_ref, s32[4]{0:T(128)S(1)} %copy-done, bf16[80,2176]{1,0:T(8,128)(2,1)S(1)} %collective-permute-done.4.pq_ref, bf16[9216,256]{1,0:T(8,128)(2,1)S(1)} %get-tuple-element.44.k_ref, bf16[128,9216]{1,0:T(8,128)(2,1)S(1)} %get-tuple-element.45.vt_ref, ...), custom_call_target="tpu_custom_call" | custom-call | flops 1 | bytes 1 | tf_op jit(solution)/shard_map/flash_far/pallas_call | solution.py:394
  189.4 0.1 collective-permute-start.8
  189.5 151.5 %flash_far.3.refs_1_ = bf16[136,1280]{1,0:T(8,128)(2,1)S(1)} custom-call(s32[2]{0:T(128)S(1)} %pad_add_fusion.me_ref, s32[4]{0:T(128)S(1)} %copy-done, bf16[80,2176]{1,0:T(8,128)(2,1)S(1)} %get-tuple-element.46.pq_ref, bf16[9216,256]{1,0:T(8,128)(2,1)S(1)} %get-tuple-element.44.k_ref, bf16[128,9216]{1,0:T(8,128)(2,1)S(1)} %get-tuple-element.45.vt_ref, ...), custom_call_target="tpu_custom_call" | custom-call | flops 1 | bytes 1 | tf_op jit(solution)/shard_map/flash_far/pallas_call | solution.py:394
  341.0 0.0 collective-permute-done.8.refs_0_
  341.0 0.5 merge.1
  341.5 0.1 collective-permute-start.9
  341.6 11.5 %collective-permute-start.10 = (bf16[40,1024]{1,0:T(8,128)(2,1)S(1)}, bf16[40,1024]{1,0:T(8,128)(2,1)S(1)}, u32[]{:S(2)}, u32[]{:S(2)}) collective-permute-start(bf16[40,1024]{1,0:T(8,128)(2,1)S(1)} %get-tuple-element.49), channel_id=1, source_target_pairs={{0,2},{1,3},{2,0},{3,1},{4,6},{5,7},{6,4},{7,5},{8,10},{9,11},{10,... | collective-permute-start | bytes 245768 | tf_op jit(solution)/shard_map/ppermute | solution.py:334
  353.1 0.5 collective-permute-start.11
  353.6 0.0 collective-permute-done.9.refs_0_
  353.6 5.8 %collective-permute-done.10.refs_1_ = bf16[40,1024]{1,0:T(8,128)(2,1)S(1)} collective-permute-done((bf16[40,1024]{1,0:T(8,128)(2,1)S(1)}, bf16[40,1024]{1,0:T(8,128)(2,1)S(1)}, u32[]{:S(2)}, u32[]{:S(2)}) %collective-permute-start.10) | collective-permute-done | bytes 81952 | tf_op jit(solution)/shard_map/ppermute | solution.py:334
  359.4 1.0 unroute.1
  (6 shorter events, 0.0 us)
Async XLA Ops:
  2.1 7.5 %collective-permute-start.3 = (bf16[2304,256]{1,0:T(8,128)(2,1)S(1)}, bf16[2304,256]{1,0:T(8,128)(2,1)S(1)}, u32[]{:S(2)}, u32[]{:S(2)}) collective-permute-start(bf16[2304,256]{1,0:T(8,128)(2,1)S(1)} %get-tuple-element.33.own_ref), channel_id=1, source_target_pairs={{0,4},{4,0},{8,12},{12,8},{16,20},{20,16},{24,28},{28,24},{1,5},{5... | collective-permute-start | bytes 3538952 | tf_op jit(solution)/shard_map/ppermute | solution.py:334
  2.6 31.8 %collective-permute-start.5 = (bf16[2304,256]{1,0:T(8,128)(2,1)S(1)}, bf16[2304,256]{1,0:T(8,128)(2,1)S(1)}, u32[]{:S(2)}, u32[]{:S(2)}) collective-permute-start(bf16[2304,256]{1,0:T(8,128)(2,1)S(1)} %get-tuple-element.33.own_ref), channel_id=1, source_target_pairs={{0,16},{4,20},{8,24},{12,28},{16,0},{20,4},{24,8},{28,12},{1,17},{... | collective-permute-start | bytes 3538952 | tf_op jit(solution)/shard_map/ppermute | solution.py:334
  5.2 7.4 %collective-permute-start = (bf16[40,1152]{1,0:T(8,128)(2,1)S(1)}, bf16[40,1152]{1,0:T(8,128)(2,1)S(1)}, u32[]{:S(2)}, u32[]{:S(2)}) collective-permute-start(bf16[40,1152]{1,0:T(8,128)(2,1)S(1)} %get-tuple-element.29), channel_id=1, source_target_pairs={{0,3},{1,2},{2,1},{3,0},{4,7},{5,6},{6,5},{7,4},{8,11},{9,10},{10,... | collective-permute-start | bytes 276488 | tf_op jit(solution)/shard_map/ppermute | solution.py:334
  8.8 8.1 %collective-permute-start.1 = (bf16[40,1152]{1,0:T(8,128)(2,1)S(1)}, bf16[40,1152]{1,0:T(8,128)(2,1)S(1)}, u32[]{:S(2)}, u32[]{:S(2)}) collective-permute-start(bf16[40,1152]{1,0:T(8,128)(2,1)S(1)} %get-tuple-element.30), channel_id=1, source_target_pairs={{0,2},{1,3},{2,0},{3,1},{4,6},{5,7},{6,4},{7,5},{8,10},{9,11},{10,... | collective-permute-start | bytes 276488 | tf_op jit(solution)/shard_map/ppermute | solution.py:334
  8.8 10.2 %copy-start = (s32[4]{0:T(128)S(1)}, s32[4]{0:T(128)}, u32[]{:S(2)}) copy-start(s32[4]{0:T(128)} %len_ref.7) | copy-start | bytes 52
  8.8 8.1 %collective-permute-start.2 = (bf16[40,1152]{1,0:T(8,128)(2,1)S(1)}, bf16[40,1152]{1,0:T(8,128)(2,1)S(1)}, u32[]{:S(2)}, u32[]{:S(2)}) collective-permute-start(bf16[40,1152]{1,0:T(8,128)(2,1)S(1)} %get-tuple-element.31), channel_id=1, source_target_pairs={{0,1},{1,0},{2,3},{3,2},{4,5},{5,4},{6,7},{7,6},{8,9},{9,8},{10,11... | collective-permute-start | bytes 276488 | tf_op jit(solution)/shard_map/ppermute | solution.py:334
  17.4 9.5 %collective-permute-start.4 = (bf16[80,2176]{1,0:T(8,128)(2,1)S(1)}, bf16[80,2176]{1,0:T(8,128)(2,1)S(1)}, u32[]{:S(2)}, u32[]{:S(2)}) collective-permute-start(bf16[80,2176]{1,0:T(8,128)(2,1)S(1)} %get-tuple-element.46.pq_ref), channel_id=1, source_target_pairs={{0,8},{4,12},{8,0},{12,4},{16,24},{20,28},{24,16},{28,20},{1,9},{5... | collective-permute-start | bytes 1044488 | tf_op jit(solution)/shard_map/ppermute | solution.py:334
  34.5 2.1 collective-permute-start.7
  34.5 2.8 collective-permute-start.6
  189.4 151.6 %collective-permute-start.8 = (bf16[136,1280]{1,0:T(8,128)(2,1)S(1)}, bf16[136,1280]{1,0:T(8,128)(2,1)S(1)}, u32[]{:S(2)}, u32[]{:S(2)}) collective-permute-start(bf16[136,1280]{1,0:T(8,128)(2,1)S(1)} %flash_far.2), channel_id=1, source_target_pairs={{0,8},{4,12},{8,0},{12,4},{16,24},{20,28},{24,16},{28,20},{1,9},{5... | collective-permute-start | bytes 1044488 | tf_op jit(solution)/shard_map/ppermute | solution.py:334
  341.5 12.1 %collective-permute-start.9 = (bf16[40,1024]{1,0:T(8,128)(2,1)S(1)}, bf16[40,1024]{1,0:T(8,128)(2,1)S(1)}, u32[]{:S(2)}, u32[]{:S(2)}) collective-permute-start(bf16[40,1024]{1,0:T(8,128)(2,1)S(1)} %get-tuple-element.48), channel_id=1, source_target_pairs={{0,3},{1,2},{2,1},{3,0},{4,7},{5,6},{6,5},{7,4},{8,11},{9,10},{10,... | collective-permute-start | bytes 245768 | tf_op jit(solution)/shard_map/ppermute | solution.py:334
  341.6 17.8 %collective-permute-start.10 = (bf16[40,1024]{1,0:T(8,128)(2,1)S(1)}, bf16[40,1024]{1,0:T(8,128)(2,1)S(1)}, u32[]{:S(2)}, u32[]{:S(2)}) collective-permute-start(bf16[40,1024]{1,0:T(8,128)(2,1)S(1)} %get-tuple-element.49), channel_id=1, source_target_pairs={{0,2},{1,3},{2,0},{3,1},{4,6},{5,7},{6,4},{7,5},{8,10},{9,11},{10,... | collective-permute-start | bytes 245768 | tf_op jit(solution)/shard_map/ppermute | solution.py:334
  353.1 6.3 %collective-permute-start.11 = (bf16[40,1024]{1,0:T(8,128)(2,1)S(1)}, bf16[40,1024]{1,0:T(8,128)(2,1)S(1)}, u32[]{:S(2)}, u32[]{:S(2)}) collective-permute-start(bf16[40,1024]{1,0:T(8,128)(2,1)S(1)} %get-tuple-element.50), channel_id=1, source_target_pairs={{0,1},{1,0},{2,3},{3,2},{4,5},{5,4},{6,7},{7,6},{8,9},{9,8},{10,11... | collective-permute-start | bytes 245768 | tf_op jit(solution)/shard_map/ppermute | solution.py:334
